TPU v7x, 32 devices: a whole 2x2x4 slice. The times are simulated.
32 devices in a mesh: section: 8 (over y, x, core), sp: 4 (over z).
Axes of the slice: x: 2, y: 2, z: 4, core: 2. Of those that a mesh axis runs over, the one named last changes fastest.
Arguments:
- resid: float32 [8, 896, 6144], P('section', 'sp'), may hold values from -1.8 to 1.8
- qkv: bfloat16 [8, 896, 3, 6144], P('section', 'sp'), may hold values from -48 to 48
- cache_kv: bfloat16 [8, 2, 2, 1344, 6144], P('section', None, None, None, 'sp'), may hold values from -6 to 6
- out_proj: bfloat16 [8, 6144, 6144], P('section', 'sp'), may hold values from -0.078125 to 0.078125
- gate: float32 [8, 2, 6144], P('section'), may hold values from 0.5 to 2
- span_ids: int32 [8], P('section'), may hold values from 3 to 39
- cache_counts: int32 [8], P('section'), may hold values from 0 to 3, as said below
- span_mask: int32 [40, 40], replicated, may hold values from 0 to 1, as said below
Outputs:
- carried: float32 [8, 896, 6144], P('section', 'sp')
Inputs may be any that keep to these rules, and one draw needn't show every extreme that they name: `cache_counts`: some section has all 3 slots filled. span_mask[i][j] is 0 for j > i and 1 for j = i.
All inputs are finite; a program needn't handle non-finite values.
Results may differ from a plain program's by a relative error of at most 0.006.
Values may be sent and summed in bfloat16 or wider, within the bound.
A program may use at most 384 MiB of HBM per device.

v0:
```python
import jax
import jax.numpy as jnp
from jax import lax
from jax.sharding import PartitionSpec as P

HDIM = 128
SPAN = 448
NCHUNK = 40
SLOTS = 3
VIDS = 2
TOKS = 896
KEYS = 1344


def passed_along(shard, axis, by):
    devices = lax.axis_size(axis)
    return lax.ppermute(shard, axis, [(i, (i + by) % devices) for i in range(devices)])


def visible_slots(span_id, filled, span_mask):
    row_mask = lax.dynamic_index_in_dim(span_mask, span_id, 0, keepdims=False)
    slot_ids = jnp.arange(SLOTS, dtype=jnp.int32)
    wanted = span_id - 1 - slot_ids
    columns = jnp.arange(NCHUNK, dtype=jnp.int32)
    looked = jnp.sum(jnp.where(columns[None, :] == wanted[:, None], row_mask[None, :], 0), axis=1)
    return (slot_ids < filled) & (looked == 1)


def far_scores(queries, cache_keys, live_slots):
    score_scale = HDIM ** (-0.5)
    scores = (
        jnp.einsum("qhe,khe->hqk", queries, cache_keys, preferred_element_type=jnp.float32)
        * score_scale
    )
    key_live = jnp.repeat(live_slots, SPAN)
    result = jnp.where(key_live[None, None, :], scores, -jnp.inf)
    return result


def mix_video(far_part, queries, own_keys, own_values, cache_values):
    score_scale = HDIM ** (-0.5)
    near_part = (
        jnp.einsum("qhe,khe->hqk", queries, own_keys, preferred_element_type=jnp.float32)
        * score_scale
    )
    scores = jnp.concatenate([far_part, near_part], axis=2)
    highest = jnp.max(scores, axis=2, keepdims=True)
    raised = jnp.exp(scores - highest)
    weights = (raised / jnp.sum(raised, axis=2, keepdims=True)).astype(jnp.bfloat16)
    values_all = jnp.concatenate([cache_values, own_values], axis=0)
    mixed = jnp.einsum("hqk,khe->qhe", weights, values_all, preferred_element_type=jnp.float32)
    return mixed.astype(jnp.bfloat16).reshape(SPAN, queries.shape[1] * HDIM)


def per_device(resid, qkv, cache_kv, out_proj, gate, span_ids, cache_counts, span_mask):
    own_rows = resid.shape[1]
    local_width = cache_kv.shape[4]
    local_heads = local_width // HDIM
    filled = cache_counts[0]
    live_slots = visible_slots(span_ids[0], filled, span_mask)
    cache_keys = cache_kv[0, 0].reshape(VIDS, KEYS, local_heads, HDIM)
    cache_values = cache_kv[0, 1].reshape(VIDS, KEYS, local_heads, HDIM)

    def score_video(inputs_one):
        return far_scores(inputs_one[0], inputs_one[1], live_slots)

    spread = lax.all_to_all(qkv[0], "sp", split_axis=2, concat_axis=0, tiled=True)
    queries = spread[:, 0].reshape(VIDS, SPAN, local_heads, HDIM)
    far_all = lax.map(score_video, (queries, cache_keys))
    own_keys = spread[:, 1].reshape(VIDS, SPAN, local_heads, HDIM)
    own_values = spread[:, 2].reshape(VIDS, SPAN, local_heads, HDIM)

    def mix_one(inputs_one):
        return mix_video(inputs_one[0], inputs_one[1], inputs_one[2], inputs_one[3], inputs_one[4])

    heads_all = lax.map(mix_one, (far_all, queries, own_keys, own_values, cache_values)).reshape(
        TOKS, local_width
    )
    projected = lax.psum_scatter(
        jnp.dot(heads_all, out_proj[0], preferred_element_type=jnp.float32),
        "sp",
        scatter_dimension=0,
        tiled=True,
    )
    device_place = lax.axis_index("sp")
    video_of = (device_place * own_rows + jnp.arange(own_rows, dtype=jnp.int32)) // SPAN
    picker = (video_of[:, None] == jnp.arange(VIDS, dtype=jnp.int32)[None, :]).astype(jnp.float32)
    gains = jnp.dot(picker, gate[0], precision=lax.Precision.HIGHEST)
    layer_out = resid[0] + gains * projected
    return passed_along(layer_out[None], "section", 1)


def solution(mesh):
    in_specs = (
        P("section", "sp", None),
        P("section", "sp", None, None),
        P("section", None, None, None, "sp"),
        P("section", "sp", None),
        P("section", None, None),
        P("section"),
        P("section"),
        P(),
    )
    out_specs = P("section", "sp", None)
    return jax.shard_map(
        per_device, mesh=mesh, in_specs=in_specs, out_specs=out_specs, check_vma=False
    )
```

profile of v0, /device:TPU:0, one launch (start us, length us, event | category | flops | bytes accessed | tf_op | source)
XLA Modules:
  0.0 1008.4 jit_solution(5154530179669752550)
XLA Ops:
  6.5 18.8 %copy.53 = bf16[1,224,3,6144]{1,2,3,0:T(4,128)(2,1)} copy(bf16[1,224,3,6144]{3,1,2,0:T(8,128)(2,1)} %param.13) | data formatting | bytes 16515072 | tf_op args[1]
  25.3 6.4 all-to-all-start
  33.0 11.3 %fusion.31 = (bf16[1,1,2,1344,1536]{4,3,2,1,0:T(8,128)(2,1)}, bf16[1,1,2,1344,1536]{4,3,2,1,0:T(8,128)(2,1)}) fusion(bf16[1,2,2,1344,1536]{4,3,2,1,0:T(8,128)(2,1)} %param.14), kind=kLoop, calls=%fused_computation.44 | loop fusion | bytes 33030144 | tf_op jit(solution)/shard_map/slice | solution.py:61
  44.4 11.8 %copy.58 = bf16[1,1,2,1344,1536]{3,4,2,1,0:T(8,128)(2,1)} copy(bf16[1,1,2,1344,1536]{4,3,2,1,0:T(8,128)(2,1)} %get-tuple-element.147) | data formatting | bytes 16515072 | tf_op jit(solution)/shard_map/slice | solution.py:61
  56.2 12.2 %copy.60 = bf16[2,1344,12,128]{3,1,2,0:T(8,128)(2,1)} copy(bf16[2,1344,12,128]{1,3,2,0:T(8,128)(2,1)} %bitcast.82) | data formatting | bytes 16515072 | tf_op jit(solution)/shard_map/while | solution.py:69
  68.3 11.8 %copy.52 = bf16[1,1,2,1344,1536]{3,4,2,1,0:T(8,128)(2,1)} copy(bf16[1,1,2,1344,1536]{4,3,2,1,0:T(8,128)(2,1)} %get-tuple-element.148) | data formatting | bytes 16515072 | tf_op jit(solution)/shard_map/slice | solution.py:62
  80.2 12.2 %copy.62 = bf16[2,1344,12,128]{3,1,2,0:T(8,128)(2,1)} copy(bf16[2,1344,12,128]{1,3,2,0:T(8,128)(2,1)} %bitcast.83) | data formatting | bytes 16515072 | tf_op jit(solution)/shard_map/while | solution.py:76
  93.2 213.0 %all-to-all-done = bf16[224,3,6144]{0,1,2:T(4,128)(2,1)} async-done(((bf16[224,3,6144]{0,1,2:T(4,128)(2,1)}), bf16[224,3,6144]{0,1,2:T(4,128)(2,1)}, u32[]{:S(2)}, u32[]{:S(2)}) %all-to-all-start) | async-done | bytes 8257568 | tf_op jit(solution)/shard_map/all_to_all | solution.py:67
  306.3 18.7 %copy.55 = bf16[4,224,3,1536]{3,1,0,2:T(8,128)(2,1)} copy(bf16[4,224,3,1536]{1,2,3,0:T(4,128)(2,1)} %bitcast.16) | data formatting | bytes 16515072 | tf_op jit(solution)/shard_map/all_to_all | solution.py:67
  325.0 5.3 fusion.32
  330.3 5.9 reshape.32
  340.6 33.7 %while.20 = (s32[]{:T(128)}, f32[2,12,448,1344]{3,2,1,0:T(8,128)}, pred[3]{0:T(512)(128)(4,1)S(1)}, bf16[2,448,12,128]{3,1,2,0:T(8,128)(2,1)}, bf16[2,1344,12,128]{3,1,2,0:T(8,128)(2,1)}, /*index=5*/s32[]{:T(128)}) while((s32[]{:T(128)}, f32[2,12,448,1344]{3,2,1,0:T(8,128)}, pred[3]{0:T(512)(128)(4,1)S(1)}, ...), condition=%wide.region_2.3_spmd, body=%wide.region_1.2_spmd.sunk | while | flops 1864138752 | bytes 35789640 | solution.py:69
  340.7 16.7 %bitcast_dynamic-update-slice_fusion.2 = f32[2,12,448,1344]{3,2,1,0:T(8,128)} fusion(f32[2,12,448,1344]{3,2,1,0:T(8,128)} %get-tuple-element.241, s32[]{:T(128)} %get-tuple-element.240, pred[1344]{0:T(1024)(128)(4,1)S(1)} %broadcast_in_dim.72, bf16[2,1344,12,128]{3,1,2,0:T(8,128)(2,1)} %get-tuple-element.250, ...), kind=kOutput, calls=%fused_computation.clone.1 | convolution fusion | flops 1864138752 | bytes 35785536 | tf_op jit(solution)/shard_map/while/body/eval_jaxpr/qhe,khe->hqk/dot_general | solution.py:32
  357.6 16.7 %bitcast_dynamic-update-slice_fusion.2 = f32[2,12,448,1344]{3,2,1,0:T(8,128)} fusion(f32[2,12,448,1344]{3,2,1,0:T(8,128)} %get-tuple-element.241, s32[]{:T(128)} %get-tuple-element.240, pred[1344]{0:T(1024)(128)(4,1)S(1)} %broadcast_in_dim.72, bf16[2,1344,12,128]{3,1,2,0:T(8,128)(2,1)} %get-tuple-element.250, ...), kind=kOutput, calls=%fused_computation.clone.1 | convolution fusion | flops 1864138752 | bytes 35785536 | tf_op jit(solution)/shard_map/while/body/eval_jaxpr/qhe,khe->hqk/dot_general | solution.py:32
  374.3 5.9 reshape.30
  380.2 4.3 copy.63
  387.8 4.3 copy.65
  392.1 149.7 %while.21 = (s32[]{:T(128)}, bf16[2,448,1536]{2,1,0:T(8,128)(2,1)}, bf16[2,1344,12,128]{3,1,2,0:T(8,128)(2,1)}, bf16[2,448,12,128]{3,1,2,0:T(8,128)(2,1)}, f32[2...) while((s32[]{:T(128)}, bf16[2,448,1536]{2,1,0:T(8,128)(2,1)}, ...), condition=%wide.region_7.8_spmd, body=%wide.region_3.7_spmd.sunk | while | flops 3173979648 | bytes 184613504 | solution.py:76
  392.1 7.4 fusion.43
  399.5 22.0 %dynamic-slice_reduce_fusion.2 = (f32[12,448]{1,0:T(8,128)S(1)}, f32[12,448,1344]{2,1,0:T(8,128)}) fusion(f32[2,12,448,1344]{3,2,1,0:T(8,128)} %get-tuple-element.272, s32[]{:T(128)} %get-tuple-element.260), kind=kLoop, calls=%fused_computation.9.clone.1 | loop fusion | flops 7219968 | bytes 57824260 | tf_op jit(solution)/shard_map/while/body/eval_jaxpr/reduce_max | solution.py:47
  421.5 20.2 %fusion.44 = f32[12,448]{1,0:T(8,128)S(1)} fusion(f32[12,448,448]{2,1,0:T(8,128)} %get-tuple-element.230, f32[12,448,1344]{2,1,0:T(8,128)} %get-tuple-element.231, f32[12,448]{1,0:T(8,128)S(1)} %reduce_max.27), kind=kLoop, calls=%fused_computation.11.clone.1 | loop fusion | flops 28896000 | bytes 38578176 | tf_op jit(solution)/shard_map/while/body/eval_jaxpr/reduce_sum | solution.py:49
  441.7 4.6 dynamic-slice_bitcast_fusion.7
  446.4 18.0 %fusion.45 = bf16[448,12,128]{2,0,1:T(8,128)(2,1)S(1)} fusion(bf16[448,12,128]{2,0,1:T(8,128)(2,1)S(1)} %dynamic-slice_bitcast_fusion.6, bf16[1344,12,128]{2,0,1:T(8,128)(2,1)} %dynamic-slice_bitcast_fusion.7, f32[12,448,448]{2,1,0:T(8,128)} %get-tuple-element.230, f32[12,448,1344]{2,1,0:T(8,128)} %get-tuple-element.231, f32[12,448]{1,0:T(8,128)S(1)} %fusion.44, ...), kind=kOutput, calls=%fused_computation.19.clone.1 | convolution fusion | flops 2516484096 | bytes 45459456 | tf_op jit(solution)/shard_map/while/body/eval_jaxpr/hqk,khe->qhe/dot_general | solution.py:51
  467.0 7.4 fusion.43
  474.4 22.0 %dynamic-slice_reduce_fusion.2 = (f32[12,448]{1,0:T(8,128)S(1)}, f32[12,448,1344]{2,1,0:T(8,128)}) fusion(f32[2,12,448,1344]{3,2,1,0:T(8,128)} %get-tuple-element.272, s32[]{:T(128)} %get-tuple-element.260), kind=kLoop, calls=%fused_computation.9.clone.1 | loop fusion | flops 7219968 | bytes 57824260 | tf_op jit(solution)/shard_map/while/body/eval_jaxpr/reduce_max | solution.py:47
  496.3 20.2 %fusion.44 = f32[12,448]{1,0:T(8,128)S(1)} fusion(f32[12,448,448]{2,1,0:T(8,128)} %get-tuple-element.230, f32[12,448,1344]{2,1,0:T(8,128)} %get-tuple-element.231, f32[12,448]{1,0:T(8,128)S(1)} %reduce_max.27), kind=kLoop, calls=%fused_computation.11.clone.1 | loop fusion | flops 28896000 | bytes 38578176 | tf_op jit(solution)/shard_map/while/body/eval_jaxpr/reduce_sum | solution.py:49
  516.6 4.6 dynamic-slice_bitcast_fusion.7
  521.2 18.0 %fusion.45 = bf16[448,12,128]{2,0,1:T(8,128)(2,1)S(1)} fusion(bf16[448,12,128]{2,0,1:T(8,128)(2,1)S(1)} %dynamic-slice_bitcast_fusion.6, bf16[1344,12,128]{2,0,1:T(8,128)(2,1)} %dynamic-slice_bitcast_fusion.7, f32[12,448,448]{2,1,0:T(8,128)} %get-tuple-element.230, f32[12,448,1344]{2,1,0:T(8,128)} %get-tuple-element.231, f32[12,448]{1,0:T(8,128)S(1)} %fusion.44, ...), kind=kOutput, calls=%fused_computation.19.clone.1 | convolution fusion | flops 2516484096 | bytes 45459456 | tf_op jit(solution)/shard_map/while/body/eval_jaxpr/hqk,khe->qhe/dot_general | solution.py:51
  541.8 24.2 %fusion.24 = f32[896,6144]{1,0:T(8,128)} fusion(bf16[896,1536]{1,0:T(8,128)(2,1)} %bitcast.85, bf16[1,1536,6144]{2,1,0:T(8,128)(2,1)} %param.15), kind=kOutput, calls=%fused_computation.29 | convolution fusion | flops 16911433728 | bytes 43646976 | tf_op jit(solution)/shard_map/dot_general | solution.py:80
  566.0 363.3 %reduce-scatter.2.cloned.1.call-done = f32[224,6144]{1,0:T(8,128)} async-done(((f32[896,6144]{1,0:T(8,128)}), f32[224,6144]{1,0:T(8,128)}) %reduce-scatter.2.cloned.1.call-update) | async-done | bytes 5505040 | tf_op jit(solution)/shard_map/reduce_scatter | solution.py:79
  929.3 6.9 fusion.27
  936.2 62.9 %collective-permute-done = f32[1,224,6144]{2,1,0:T(8,128)S(1)} collective-permute-done((f32[1,224,6144]{2,1,0:T(8,128)S(1)}, f32[1,224,6144]{2,1,0:T(8,128)S(1)}, u32[]{:S(2)}, u32[]{:S(2)}) %collective-permute-start) | collective-permute-done | bytes 5505056 | tf_op jit(solution)/shard_map/ppermute | solution.py:17
  (33 shorter events, 16.7 us)
Async XLA Ops:
  6.5 922.7 %copy-start = (f32[1,2,6144]{2,1,0:T(2,128)S(1)}, f32[1,2,6144]{2,1,0:T(2,128)}, u32[]{:S(2)}) copy-start(f32[1,2,6144]{2,1,0:T(2,128)} %param.16) | copy-start | bytes 147460
  25.3 281.0 %all-to-all-start = ((bf16[224,3,6144]{0,1,2:T(4,128)(2,1)}), bf16[224,3,6144]{0,1,2:T(4,128)(2,1)}, u32[]{:S(2)}, u32[]{:S(2)}) async-start(bf16[224,3,6144]{0,1,2:T(4,128)(2,1)} %bitcast.81), calls=%async_computation | async-start | bytes 25165824 | tf_op jit(solution)/shard_map/all_to_all | solution.py:67
  31.7 897.6 %reduce-scatter.2.cloned.1.call-start = ((), (), s32[]{:S(2)}) async-start(), calls=%async_computation.2 | async-start | bytes 27525120 | tf_op jit(solution)/shard_map/reduce_scatter | solution.py:79
  441.7 4.6 copy-start.1
  516.5 4.6 copy-start.1
  936.1 62.9 %collective-permute-start = (f32[1,224,6144]{2,1,0:T(8,128)S(1)}, f32[1,224,6144]{2,1,0:T(8,128)S(1)}, u32[]{:S(2)}, u32[]{:S(2)}) collective-permute-start(f32[1,224,6144]{2,1,0:T(8,128)S(1)} %fusion.27), channel_id=1, source_target_pairs={{0,4},{4,8},{8,12},{12,16},{16,20},{20,24},{24,28},{28,0},{1,5},{5... | collective-permute-start | bytes 16515080 | tf_op jit(solution)/shard_map/ppermute | solution.py:17
Sparse Core Ops, SparseCore 0:
  566.1 363.1 reduce-scatter.1
where the time goes:
time: 1010 us
  waiting for transfers between devices  639 us (63%)
  local copies, waits for them, and re-layouts  148 us (15%)
  matrix products  115 us (11%)
  other arithmetic  84.6 us (8%)
  between operations  14.8 us (1%)
    reduce_scatter x1, waiting for transfers between devices, per_device(): lax.psum_scatter(jnp.dot(heads_all, out_proj[0], preferred_element_type=j...  363 us
    all_to_all x1, waiting for transfers between devices, per_device(): lax.all_to_all(qkv[0], 'sp', split_axis=2, concat_axis=0, tiled=True)  213 us
    ppermute x1, waiting for transfers between devices, passed_along(): lax.ppermute(shard, axis, [(i, (i + by) % devices) for i in range(devices)])  62.9 us
    reduce_max x4, other arithmetic, mix_video(): highest = jnp.max(scores, axis=2, keepdims=True)  43.9 us
    reduce_sum x2, other arithmetic, mix_video(): jnp.sum(raised, axis=2, keepdims=True)  40.4 us
    dot_general x2, matrix products, mix_video(): jnp.einsum('hqk,khe->qhe', weights, values_all, preferred_element_type=jn...  36 us
    dot_general x2, matrix products, far_scores(): jnp.einsum('qhe,khe->hqk', queries, cache_keys, preferred_element_type=jn...  33.4 us
    dot_general x1, matrix products, per_device(): jnp.dot(heads_all, out_proj[0], preferred_element_type=jnp.float32)  24.2 us
  transfers between devices with their start and end apart: 3, of which 3 were waited for; matrix products, arithmetic and copies ran while one was open for 6% of the time, Pallas kernels for 0%

commit v1 on v0

v1 whole, which is shorter than its diff:
```python
import math

import jax
import jax.numpy as jnp
from jax import lax
from jax.experimental import pallas as pl
from jax.experimental.pallas import tpu as pltpu
from jax.sharding import PartitionSpec as P

HDIM = 128
SPAN = 448
NCHUNK = 40
SLOTS = 3
VIDS = 2
TOKS = 896
KEYS = 1344
PAIR = 2 * HDIM
FLOOR = -3.0e38
SCALE = HDIM ** (-0.5) * math.log2(math.e)
COLS = 1024


def swapped(shard, axis, bit):
    devices = lax.axis_size(axis)
    return lax.ppermute(shard, axis, [(i, i ^ bit) for i in range(devices)])


def passed_along(shard, axis, by):
    devices = lax.axis_size(axis)
    return lax.ppermute(shard, axis, [(i, (i + by) % devices) for i in range(devices)])


def visible_slots(span_id, filled, span_mask):
    row_mask = lax.dynamic_index_in_dim(span_mask, span_id, 0, keepdims=False)
    slot_ids = jnp.arange(SLOTS, dtype=jnp.int32)
    wanted = span_id - 1 - slot_ids
    columns = jnp.arange(NCHUNK, dtype=jnp.int32)
    looked = jnp.sum(jnp.where(columns[None, :] == wanted[:, None], row_mask[None, :], 0), axis=1)
    return (slot_ids < filled) & (looked == 1)


def dot_t(left, right):
    return lax.dot_general(left, right, (((1,), (1,)), ((), ())), preferred_element_type=jnp.float32)


def far_kernel(q_ref, k_ref, v_ref, bias_ref, acc_ref, stat_ref):
    for head in range(2):
        cols = slice(head * HDIM, (head + 1) * HDIM)
        scores = dot_t(q_ref[:, cols], k_ref[0, 0, 0, :, cols]) + bias_ref[0:1, :]
        highest = jnp.maximum(jnp.max(scores, axis=1, keepdims=True), FLOOR)
        raised = jnp.exp2(scores * SCALE - highest * SCALE)
        total = jnp.sum(raised, axis=1, keepdims=True)
        acc_ref[:, cols] = jnp.dot(
            raised.astype(jnp.bfloat16), v_ref[0, 0, 0, :, cols], preferred_element_type=jnp.float32
        )
        lane = lax.broadcasted_iota(jnp.int32, (SPAN, HDIM), 1)
        stat_ref[:, cols] = jnp.where(lane < HDIM // 2, highest, total)


def near_kernel(q_ref, k_ref, v_ref, acc_ref, stat_ref, out_ref):
    for head in range(2):
        cols = slice(head * HDIM, (head + 1) * HDIM)
        scores = dot_t(q_ref[:, cols], k_ref[:, cols])
        far_high = stat_ref[:, head * HDIM : head * HDIM + 1]
        far_total = stat_ref[:, head * HDIM + HDIM // 2 : head * HDIM + HDIM // 2 + 1]
        highest = jnp.maximum(jnp.max(scores, axis=1, keepdims=True), far_high)
        raised = jnp.exp2(scores * SCALE - highest * SCALE)
        fade = jnp.exp2((far_high - highest) * SCALE)
        total = jnp.sum(raised, axis=1, keepdims=True) + far_total * fade
        mixed = jnp.dot(raised.astype(jnp.bfloat16), v_ref[:, cols], preferred_element_type=jnp.float32)
        mixed = (mixed + acc_ref[:, cols] * fade) / total
        out_ref[:, cols] = mixed.astype(jnp.bfloat16)


def far_mix(queries, cache_kv, live_slots):
    width = queries.shape[1]
    bias = jnp.where(jnp.repeat(live_slots, SPAN), 0.0, -jnp.inf).astype(jnp.float32)
    bias = jnp.broadcast_to(bias[None, :], (8, KEYS))
    block = pl.BlockSpec((SPAN, PAIR), lambda b, h: (b, h))
    return pl.pallas_call(
        far_kernel,
        grid=(VIDS, width // PAIR),
        in_specs=[
            block,
            pl.BlockSpec((1, 1, 1, KEYS, PAIR), lambda b, h: (0, 0, b, 0, h)),
            pl.BlockSpec((1, 1, 1, KEYS, PAIR), lambda b, h: (0, 1, b, 0, h)),
            pl.BlockSpec((8, KEYS), lambda b, h: (0, 0)),
        ],
        out_specs=[block, block],
        out_shape=[jax.ShapeDtypeStruct((TOKS, width), jnp.float32)] * 2,
        compiler_params=pltpu.CompilerParams(vmem_limit_bytes=40 * 1024 * 1024),
        cost_estimate=pl.CostEstimate(
            flops=4 * TOKS * KEYS * width * 4,
            bytes_accessed=2 * VIDS * KEYS * width * 2 + TOKS * width * 10,
            transcendentals=TOKS * KEYS * (width // HDIM),
        ),
    )(queries, cache_kv, cache_kv, bias)


def near_mix(queries, keys, values, acc, stat):
    width = queries.shape[1]
    block = pl.BlockSpec((SPAN, PAIR), lambda b, h: (b, h))
    return pl.pallas_call(
        near_kernel,
        grid=(VIDS, width // PAIR),
        in_specs=[block] * 5,
        out_specs=block,
        out_shape=jax.ShapeDtypeStruct((TOKS, width), jnp.bfloat16),
        compiler_params=pltpu.CompilerParams(vmem_limit_bytes=40 * 1024 * 1024),
        cost_estimate=pl.CostEstimate(
            flops=4 * TOKS * SPAN * width * 4,
            bytes_accessed=TOKS * width * 16,
            transcendentals=TOKS * SPAN * (width // HDIM),
        ),
    )(queries, keys, values, acc, stat)


def heads_gathered(local, place, devices):
    rows, width = local.shape[0], local.shape[1] // devices
    whole = jnp.zeros((rows * devices, width), local.dtype)
    for bit in range(devices):
        other = place ^ bit
        piece = lax.dynamic_slice(local, (0, other * width), (rows, width))
        if bit:
            piece = swapped(piece, "sp", bit)
        whole = lax.dynamic_update_slice(whole, piece, (other * rows, 0))
    return whole


def per_device(resid, qkv, cache_kv, out_proj, gate, span_ids, cache_counts, span_mask):
    own_rows = resid.shape[1]
    model = resid.shape[2]
    devices = lax.axis_size("sp")
    place = lax.axis_index("sp")
    live_slots = visible_slots(span_ids[0], cache_counts[0], span_mask)

    queries = heads_gathered(qkv[0, :, 0], place, devices)
    acc, stat = far_mix(queries, cache_kv, live_slots)
    keys = heads_gathered(qkv[0, :, 1], place, devices)
    values = heads_gathered(qkv[0, :, 2], place, devices)
    heads_all = near_mix(queries, keys, values, acc, stat)

    resid_prev = passed_along(resid[0], "section", 1)
    gate_prev = passed_along(gate[0], "section", 1)
    video_of = (place * own_rows + jnp.arange(own_rows, dtype=jnp.int32)) // SPAN

    row_blocks = [
        lax.dynamic_slice(heads_all, ((place ^ bit) * own_rows, 0), (own_rows, heads_all.shape[1]))
        for bit in range(devices)
    ]
    odd = jnp.concatenate(row_blocks[1::2], axis=0)
    even = jnp.concatenate(row_blocks[0::2], axis=0)
    pieces = []
    for start in range(0, model, COLS):
        proj = out_proj[0, :, start : start + COLS]
        sent = jnp.dot(odd, proj, preferred_element_type=jnp.float32).astype(jnp.bfloat16)
        summed = jnp.dot(even, proj, preferred_element_type=jnp.float32)
        summed = summed + swapped(sent, "sp", 1).astype(jnp.float32)
        blocks = [summed[i * own_rows : (i + 1) * own_rows] for i in range(devices // 2)]
        bit = 2
        while bit < devices:
            sent = jnp.concatenate(blocks[1::2], axis=0).astype(jnp.bfloat16)
            arrived = swapped(sent, "sp", bit).astype(jnp.float32)
            kept = blocks[0::2]
            blocks = [kept[i] + arrived[i * own_rows : (i + 1) * own_rows] for i in range(len(kept))]
            bit *= 2
        moved = passed_along(blocks[0].astype(jnp.bfloat16), "section", 1).astype(jnp.float32)
        gate_cols = gate_prev[:, start : start + COLS]
        gains = jnp.where((video_of == 0)[:, None], gate_cols[0:1], gate_cols[1:2])
        pieces.append(resid_prev[:, start : start + COLS] + gains * moved)
    return jnp.concatenate(pieces, axis=1)[None]


def solution(mesh):
    in_specs = (
        P("section", "sp", None),
        P("section", "sp", None, None),
        P("section", None, None, None, "sp"),
        P("section", "sp", None),
        P("section", None, None),
        P("section"),
        P("section"),
        P(),
    )
    out_specs = P("section", "sp", None)
    return jax.shard_map(
        per_device, mesh=mesh, in_specs=in_specs, out_specs=out_specs, check_vma=False
    )
```

time: 1010 us -> 491 us (0.49)
  waiting for transfers between devices: 639 us -> 292 us
  local copies, waits for them, and re-layouts: 148 us -> 30.4 us
  other arithmetic: 84.6 us -> 2.1 us
  matrix products: 115 us -> 37.7 us
  Pallas kernels: 0 us -> 69.8 us
  starting transfers between devices: 6.47 us -> 56.3 us
  between operations: 14.8 us -> 1.96 us
    reduce_scatter x1 -> x0, waiting for transfers between devices: 363 us -> none  [per_device(): lax.psum_scatter(jnp.dot(heads_all, out_proj[0], preferred_element_type=j...]
    ppermute x0 -> x21, waiting for transfers between devices: none -> 267 us  [swapped(): return lax.ppermute(shard, axis, [(i, i ^ bit) for i in range(devices)])]
    all_to_all x1 -> x0, waiting for transfers between devices: 213 us -> none  [per_device(): lax.all_to_all(qkv[0], 'sp', split_axis=2, concat_axis=0, tiled=True)]
    dot_general x8 -> x12, matrix products: 115 us -> 37.7 us  [the longest x6 21.3 us: per_device(): summed = jnp.dot(even, proj, preferred_element_type=jnp.float32)]
    pallas_call x0 -> x2, Pallas kernels: none -> 69.8 us  [the longest x1 36.8 us: near_mix(): pl.pallas_call(near_kernel, grid=(VIDS, width // PAIR), in_specs=[block]...]
    ppermute x0 -> x21, starting transfers between devices: none -> 53.8 us  [swapped(): return lax.ppermute(shard, axis, [(i, i ^ bit) for i in range(devices)])]
    reduce_max x4 -> x0, other arithmetic: 43.9 us -> none  [mix_video(): highest = jnp.max(scores, axis=2, keepdims=True)]
    reduce_sum x2 -> x0, other arithmetic: 40.4 us -> none  [mix_video(): jnp.sum(raised, axis=2, keepdims=True)]
  transfers between devices with their start and end apart: 3 -> 29, of which waited for: 3 -> 14; matrix products, arithmetic and copies ran while one was open for 6% -> 11% of each run, Pallas kernels for 0% -> 14%
where the time goes in v1:
time: 491 us; the launch traced here: 490 us
  waiting for transfers between devices  292 us (59%)
  Pallas kernels  69.8 us (14%)
  starting transfers between devices  56.3 us (11%)
  matrix products  37.7 us (8%)
  local copies, waits for them, and re-layouts  30.4 us (6%)
    ppermute x21, waiting for transfers between devices, swapped(): return lax.ppermute(shard, axis, [(i, i ^ bit) for i in range(devices)])  267 us
    ppermute x21, starting transfers between devices, swapped(): return lax.ppermute(shard, axis, [(i, i ^ bit) for i in range(devices)])  53.8 us
    pallas_call x1, Pallas kernels, near_mix(): pl.pallas_call(near_kernel, grid=(VIDS, width // PAIR), in_specs=[block]...  36.8 us
    pallas_call x1, Pallas kernels, far_mix(): pl.pallas_call(far_kernel, grid=(VIDS, width // PAIR), in_specs=[block, p...  33 us
    ppermute x8, waiting for transfers between devices, passed_along(): lax.ppermute(shard, axis, [(i, (i + by) % devices) for i in range(devices)])  25.2 us
    dot_general x6, matrix products, per_device(): summed = jnp.dot(even, proj, preferred_element_type=jnp.float32)  21.3 us
    dot_general x6, matrix products, per_device(): jnp.dot(odd, proj, preferred_element_type=jnp.float32).astype(jnp.bfloat16)  16.3 us
    dynamic_update_slice x12, local copies, waits for them, and re-layouts, heads_gathered(): whole = lax.dynamic_update_slice(whole, piece, (other * rows, 0))  10.7 us
  transfers between devices with their start and end apart: 29, of which 14 were waited for; matrix products, arithmetic and copies ran while one was open for 11% of the time, Pallas kernels for 14%

profile of v1, /device:TPU:0, one launch (start us, length us, event | category | flops | bytes accessed | tf_op | source)
XLA Modules:
  0.0 490.2 jit_solution(12184131372741522548)
XLA Ops:
  0.0 5.4 %fusion.80 = (bf16[1,224,1,6144]{3,1,2,0:T(8,128)(2,1)}, bf16[1,224,1,6144]{3,1,2,0:T(8,128)(2,1)S(1)}, bf16[1,224,1,6144]{3,1,2,0:T(8,128)(2,1)}) fusion(bf16[1,224,3,6144]{3,1,2,0:T(8,128)(2,1)} %param.9), kind=kLoop, calls=%fused_computation.113 | loop fusion | bytes 16515072 | tf_op jit(solution)/shard_map/slice | solution.py:140
  5.5 3.7 dynamic-slice_bitcast_fusion
  9.2 3.0 collective-permute-start.8
  26.4 4.0 collective-permute-start.4
  30.4 41.1 %collective-permute-done.2 = bf16[224,1536]{1,0:T(8,128)(2,1)} collective-permute-done((bf16[224,1536]{1,0:T(8,128)(2,1)}, bf16[224,1536]{1,0:T(8,128)(2,1)}, u32[]{:S(2)}, u32[]{:S(2)}) %collective-permute-start.2) | collective-permute-done | bytes 688160 | tf_op jit(solution)/shard_map/ppermute | solution.py:25
  71.4 3.2 collective-permute-start.10
  75.8 29.8 %collective-permute-done.3 = bf16[224,1536]{1,0:T(8,128)(2,1)} collective-permute-done((bf16[224,1536]{1,0:T(8,128)(2,1)}, bf16[224,1536]{1,0:T(8,128)(2,1)}, u32[]{:S(2)}, u32[]{:S(2)}) %collective-permute-start.3) | collective-permute-done | bytes 688160 | tf_op jit(solution)/shard_map/ppermute | solution.py:25
  106.8 15.1 %collective-permute-start.6 = (bf16[224,1536]{1,0:T(8,128)(2,1)S(1)}, bf16[224,1536]{1,0:T(8,128)(2,1)S(1)}, u32[]{:S(2)}, u32[]{:S(2)}) collective-permute-start(bf16[224,1536]{1,0:T(8,128)(2,1)S(1)} %copy-done.10), channel_id=1, source_target_pairs={{0,2},{1,3},{2,0},{3,1},{4,6},{5,7},{6,4},{7,5},{8,10},{9,11},{10,... | collective-permute-start | bytes 2064392 | tf_op jit(solution)/shard_map/ppermute | solution.py:25
  121.9 33.0 %shard_map.82 = (f32[896,1536]{1,0:T(8,128)S(1)}, f32[896,1536]{1,0:T(8,128)S(1)}) custom-call(bf16[896,1536]{1,0:T(8,128)(2,1)S(1)} %constant_dynamic-update-slice_fusion.6.q_ref, bf16[1,2,2,1344,1536]{4,3,2,1,0:T(8,128)(2,1)} %v_ref.1, bf16[1,2,2,1344,1536]{4,3,2,1,0:T(8,128)(2,1)} %v_ref.1, f32[8,1344]{1,0:T(8,128)S(1)} %broadcast_in_dim.167.bias_ref), custom_call_target="tpu_custom_call" | custom-call | flops 29595009024 | bytes 30277632 | tf_op jit(solution)/shard_map/pallas_call | solution.py:80
  162.7 16.5 %collective-permute-done.6 = bf16[224,1536]{1,0:T(8,128)(2,1)S(1)} collective-permute-done((bf16[224,1536]{1,0:T(8,128)(2,1)S(1)}, bf16[224,1536]{1,0:T(8,128)(2,1)S(1)}, u32[]{:S(2)}, u32[]{:S(2)}) %collective-permute-start.6) | collective-permute-done | bytes 688160 | tf_op jit(solution)/shard_map/ppermute | solution.py:25
  179.4 36.8 %shard_map.83 = bf16[896,1536]{1,0:T(8,128)(2,1)S(1)} custom-call(bf16[896,1536]{1,0:T(8,128)(2,1)S(1)} %constant_dynamic-update-slice_fusion.6.q_ref, bf16[896,1536]{1,0:T(8,128)(2,1)S(1)} %constant_dynamic-update-slice_fusion.3.k_ref, bf16[896,1536]{1,0:T(8,128)(2,1)S(1)} %constant_dynamic-update-slice_fusion.v_ref, f32[896,1536]{1,0:T(8,128)} %copy-done.6, ...), custom_call_target="tpu_custom_call" | custom-call | flops 9865003008 | bytes 22020096 | tf_op jit(solution)/shard_map/pallas_call | solution.py:103
  216.4 3.7 fusion.51
  220.1 4.2 fusion.48
  224.3 3.7 fusion.45
  228.0 13.9 %collective-permute-start.26 = (bf16[448,1024]{1,0:T(8,128)(2,1)S(1)}, bf16[448,1024]{1,0:T(8,128)(2,1)S(1)}, u32[]{:S(2)}, u32[]{:S(2)}) collective-permute-start(bf16[448,1024]{1,0:T(8,128)(2,1)S(1)} %fusion.51), channel_id=1, source_target_pairs={{0,1},{1,0},{2,3},{3,2},{4,5},{5,4},{6,7},{7,6},{8,9},{9,8},{10,11... | collective-permute-start | bytes 2752520 | tf_op jit(solution)/shard_map/ppermute | solution.py:25
  248.9 14.3 %collective-permute-done.26 = bf16[448,1024]{1,0:T(8,128)(2,1)S(1)} collective-permute-done((bf16[448,1024]{1,0:T(8,128)(2,1)S(1)}, bf16[448,1024]{1,0:T(8,128)(2,1)S(1)}, u32[]{:S(2)}, u32[]{:S(2)}) %collective-permute-start.26) | collective-permute-done | bytes 917536 | tf_op jit(solution)/shard_map/ppermute | solution.py:25
  265.2 3.5 convert_add_fusion
  268.8 14.0 %collective-permute-done.23 = bf16[448,1024]{1,0:T(8,128)(2,1)S(1)} collective-permute-done((bf16[448,1024]{1,0:T(8,128)(2,1)S(1)}, bf16[448,1024]{1,0:T(8,128)(2,1)S(1)}, u32[]{:S(2)}, u32[]{:S(2)}) %collective-permute-start.23) | collective-permute-done | bytes 917536 | tf_op jit(solution)/shard_map/ppermute | solution.py:25
  284.8 3.5 convert_add_fusion.1
  288.4 19.0 %collective-permute-done.20 = bf16[448,1024]{1,0:T(8,128)(2,1)S(1)} collective-permute-done((bf16[448,1024]{1,0:T(8,128)(2,1)S(1)}, bf16[448,1024]{1,0:T(8,128)(2,1)S(1)}, u32[]{:S(2)}, u32[]{:S(2)}) %collective-permute-start.20) | collective-permute-done | bytes 917536 | tf_op jit(solution)/shard_map/ppermute | solution.py:25
  307.8 3.5 convert_add_fusion.2
  311.4 25.5 %collective-permute-done.17 = bf16[448,1024]{1,0:T(8,128)(2,1)S(1)} collective-permute-done((bf16[448,1024]{1,0:T(8,128)(2,1)S(1)}, bf16[448,1024]{1,0:T(8,128)(2,1)S(1)}, u32[]{:S(2)}, u32[]{:S(2)}) %collective-permute-start.17) | collective-permute-done | bytes 917536 | tf_op jit(solution)/shard_map/ppermute | solution.py:25
  337.3 3.5 convert_add_fusion.3
  340.9 21.1 %collective-permute-done.14 = bf16[448,1024]{1,0:T(8,128)(2,1)S(1)} collective-permute-done((bf16[448,1024]{1,0:T(8,128)(2,1)S(1)}, bf16[448,1024]{1,0:T(8,128)(2,1)S(1)}, u32[]{:S(2)}, u32[]{:S(2)}) %collective-permute-start.14) | collective-permute-done | bytes 917536 | tf_op jit(solution)/shard_map/ppermute | solution.py:25
  362.0 3.7 convert_add_fusion.4
  365.8 14.9 %collective-permute-done.11 = bf16[448,1024]{1,0:T(8,128)(2,1)S(1)} collective-permute-done((bf16[448,1024]{1,0:T(8,128)(2,1)S(1)}, bf16[448,1024]{1,0:T(8,128)(2,1)S(1)}, u32[]{:S(2)}, u32[]{:S(2)}) %collective-permute-start.11) | collective-permute-done | bytes 917536 | tf_op jit(solution)/shard_map/ppermute | solution.py:25
  380.6 3.5 convert_add_fusion.5
  387.6 42.9 %collective-permute-done.21 = bf16[224,1024]{1,0:T(8,128)(2,1)S(1)} collective-permute-done((bf16[224,1024]{1,0:T(8,128)(2,1)S(1)}, bf16[224,1024]{1,0:T(8,128)(2,1)S(1)}, u32[]{:S(2)}, u32[]{:S(2)}) %collective-permute-start.21) | collective-permute-done | bytes 458784 | tf_op jit(solution)/shard_map/ppermute | solution.py:25
  430.7 27.7 %collective-permute-done.12 = bf16[224,1024]{1,0:T(8,128)(2,1)S(1)} collective-permute-done((bf16[224,1024]{1,0:T(8,128)(2,1)S(1)}, bf16[224,1024]{1,0:T(8,128)(2,1)S(1)}, u32[]{:S(2)}, u32[]{:S(2)}) %collective-permute-start.12) | collective-permute-done | bytes 458784 | tf_op jit(solution)/shard_map/ppermute | solution.py:25
  460.5 11.6 %collective-permute-done.13 = bf16[224,1024]{1,0:T(8,128)(2,1)S(1)} collective-permute-done((bf16[224,1024]{1,0:T(8,128)(2,1)S(1)}, bf16[224,1024]{1,0:T(8,128)(2,1)S(1)}, u32[]{:S(2)}, u32[]{:S(2)}) %collective-permute-start.13) | collective-permute-done | bytes 458784 | tf_op jit(solution)/shard_map/ppermute | solution.py:30
  473.0 4.0 collective-permute-done.16
  477.2 9.6 %collective-permute-done.19 = bf16[224,1024]{1,0:T(8,128)(2,1)S(1)} collective-permute-done((bf16[224,1024]{1,0:T(8,128)(2,1)S(1)}, bf16[224,1024]{1,0:T(8,128)(2,1)S(1)}, u32[]{:S(2)}, u32[]{:S(2)}) %collective-permute-start.19) | collective-permute-done | bytes 458784 | tf_op jit(solution)/shard_map/ppermute | solution.py:30
  (122 shorter events, 45.3 us)
Async XLA Ops:
  9.2 148.2 %collective-permute-start.8 = (bf16[224,1536]{1,0:T(8,128)(2,1)}, bf16[224,1536]{1,0:T(8,128)(2,1)}, u32[]{:S(2)}, u32[]{:S(2)}) collective-permute-start(bf16[224,1536]{1,0:T(8,128)(2,1)} %get-tuple-element.18), channel_id=1, source_target_pairs={{0,1},{1,0},{2,3},{3,2},{4,5},{5,4},{6,7},{7,6},{8,9},{9,8},{10,11... | collective-permute-start | bytes 2064392 | tf_op jit(solution)/shard_map/ppermute | solution.py:25
  12.2 149.1 %collective-permute-start.9 = (bf16[224,1536]{1,0:T(8,128)(2,1)}, bf16[224,1536]{1,0:T(8,128)(2,1)}, u32[]{:S(2)}, u32[]{:S(2)}) collective-permute-start(bf16[224,1536]{1,0:T(8,128)(2,1)} %get-tuple-element.17), channel_id=1, source_target_pairs={{0,2},{1,3},{2,0},{3,1},{4,6},{5,7},{6,4},{7,5},{8,10},{9,11},{10,... | collective-permute-start | bytes 2064392 | tf_op jit(solution)/shard_map/ppermute | solution.py:25
  16.2 55.3 %collective-permute-start.2 = (bf16[224,1536]{1,0:T(8,128)(2,1)}, bf16[224,1536]{1,0:T(8,128)(2,1)}, u32[]{:S(2)}, u32[]{:S(2)}) collective-permute-start(bf16[224,1536]{1,0:T(8,128)(2,1)} %get-tuple-element.24), channel_id=1, source_target_pairs={{0,1},{1,0},{2,3},{3,2},{4,5},{5,4},{6,7},{7,6},{8,9},{9,8},{10,11... | collective-permute-start | bytes 2064392 | tf_op jit(solution)/shard_map/ppermute | solution.py:25
  16.6 89.0 %collective-permute-start.3 = (bf16[224,1536]{1,0:T(8,128)(2,1)}, bf16[224,1536]{1,0:T(8,128)(2,1)}, u32[]{:S(2)}, u32[]{:S(2)}) collective-permute-start(bf16[224,1536]{1,0:T(8,128)(2,1)} %get-tuple-element.23), channel_id=1, source_target_pairs={{0,2},{1,3},{2,0},{3,1},{4,6},{5,7},{6,4},{7,5},{8,10},{9,11},{10,... | collective-permute-start | bytes 2064392 | tf_op jit(solution)/shard_map/ppermute | solution.py:25
  16.6 9.8 %collective-permute-start.1 = (f32[2,6144]{1,0:T(2,128)}, f32[2,6144]{1,0:T(2,128)S(1)}, u32[]{:S(2)}, u32[]{:S(2)}) collective-permute-start(f32[2,6144]{1,0:T(2,128)} %bitcast.1), channel_id=1, source_target_pairs={{0,4},{4,8},{8,12},{12,16},{16,20},{20,24},{24,28},{28,0},{1,5},{5... | collective-permute-start | bytes 147464 | tf_op jit(solution)/shard_map/ppermute | solution.py:30
  26.4 80.4 %copy-start.10 = (bf16[224,1536]{1,0:T(8,128)(2,1)S(1)}, bf16[224,1536]{1,0:T(8,128)(2,1)}, u32[]{:S(2)}) copy-start(bf16[224,1536]{1,0:T(8,128)(2,1)} %get-tuple-element.20) | copy-start | bytes 2064388
  26.4 80.4 %collective-permute-start.4 = (bf16[224,1536]{1,0:T(8,128)(2,1)}, bf16[224,1536]{1,0:T(8,128)(2,1)S(1)}, u32[]{:S(2)}, u32[]{:S(2)}) collective-permute-start(bf16[224,1536]{1,0:T(8,128)(2,1)} %get-tuple-element.22), channel_id=1, source_target_pairs={{0,3},{1,2},{2,1},{3,0},{4,7},{5,6},{6,5},{7,4},{8,11},{9,10},{10,... | collective-permute-start | bytes 2064392 | tf_op jit(solution)/shard_map/ppermute | solution.py:25
  71.4 91.1 %collective-permute-start.10 = (bf16[224,1536]{1,0:T(8,128)(2,1)S(1)}, bf16[224,1536]{1,0:T(8,128)(2,1)S(1)}, u32[]{:S(2)}, u32[]{:S(2)}) collective-permute-start(bf16[224,1536]{1,0:T(8,128)(2,1)S(1)} %get-tuple-element.16), channel_id=1, source_target_pairs={{0,3},{1,2},{2,1},{3,0},{4,7},{5,6},{6,5},{7,4},{8,11},{9,10},{10,... | collective-permute-start | bytes 2064392 | tf_op jit(solution)/shard_map/ppermute | solution.py:25
  105.6 57.0 %collective-permute-start.5 = (bf16[224,1536]{1,0:T(8,128)(2,1)}, bf16[224,1536]{1,0:T(8,128)(2,1)S(1)}, u32[]{:S(2)}, u32[]{:S(2)}) collective-permute-start(bf16[224,1536]{1,0:T(8,128)(2,1)} %get-tuple-element.21), channel_id=1, source_target_pairs={{0,1},{1,0},{2,3},{3,2},{4,5},{5,4},{6,7},{7,6},{8,9},{9,8},{10,11... | collective-permute-start | bytes 2064392 | tf_op jit(solution)/shard_map/ppermute | solution.py:25
  106.8 72.5 %collective-permute-start.6 = (bf16[224,1536]{1,0:T(8,128)(2,1)S(1)}, bf16[224,1536]{1,0:T(8,128)(2,1)S(1)}, u32[]{:S(2)}, u32[]{:S(2)}) collective-permute-start(bf16[224,1536]{1,0:T(8,128)(2,1)S(1)} %copy-done.10), channel_id=1, source_target_pairs={{0,2},{1,3},{2,0},{3,1},{4,6},{5,7},{6,4},{7,5},{8,10},{9,11},{10,... | collective-permute-start | bytes 2064392 | tf_op jit(solution)/shard_map/ppermute | solution.py:25
  121.9 35.5 %copy-start.9 = (bf16[224,1536]{1,0:T(8,128)(2,1)S(1)}, bf16[224,1536]{1,0:T(8,128)(2,1)}, u32[]{:S(2)}) copy-start(bf16[224,1536]{1,0:T(8,128)(2,1)} %get-tuple-element.19) | copy-start | bytes 2064388
  121.9 36.9 %copy-start.3 = (bf16[896,1536]{1,0:T(8,128)(2,1)S(1)}, bf16[896,1536]{1,0:T(8,128)(2,1)}, u32[]{:S(2)}) copy-start(bf16[896,1536]{1,0:T(8,128)(2,1)} %copy-done.2) | copy-start | bytes 8257540
  157.4 21.9 %collective-permute-start.7 = (bf16[224,1536]{1,0:T(8,128)(2,1)S(1)}, bf16[224,1536]{1,0:T(8,128)(2,1)S(1)}, u32[]{:S(2)}, u32[]{:S(2)}) collective-permute-start(bf16[224,1536]{1,0:T(8,128)(2,1)S(1)} %copy-done.9), channel_id=1, source_target_pairs={{0,3},{1,2},{2,1},{3,0},{4,7},{5,6},{6,5},{7,4},{8,11},{9,10},{10,... | collective-permute-start | bytes 2064392 | tf_op jit(solution)/shard_map/ppermute | solution.py:25
  161.3 310.8 %collective-permute-start = (f32[224,6144]{1,0:T(8,128)}, f32[224,6144]{1,0:T(8,128)S(1)}, u32[]{:S(2)}, u32[]{:S(2)}) collective-permute-start(f32[224,6144]{1,0:T(8,128)} %bitcast.116), channel_id=1, source_target_pairs={{0,4},{4,8},{8,12},{12,16},{16,20},{20,24},{24,28},{28,0},{1,5},{5... | collective-permute-start | bytes 16515080 | tf_op jit(solution)/shard_map/ppermute | solution.py:30
  228.0 35.2 %collective-permute-start.26 = (bf16[448,1024]{1,0:T(8,128)(2,1)S(1)}, bf16[448,1024]{1,0:T(8,128)(2,1)S(1)}, u32[]{:S(2)}, u32[]{:S(2)}) collective-permute-start(bf16[448,1024]{1,0:T(8,128)(2,1)S(1)} %fusion.51), channel_id=1, source_target_pairs={{0,1},{1,0},{2,3},{3,2},{4,5},{5,4},{6,7},{7,6},{8,9},{9,8},{10,11... | collective-permute-start | bytes 2752520 | tf_op jit(solution)/shard_map/ppermute | solution.py:25
  243.5 39.3 %collective-permute-start.23 = (bf16[448,1024]{1,0:T(8,128)(2,1)S(1)}, bf16[448,1024]{1,0:T(8,128)(2,1)S(1)}, u32[]{:S(2)}, u32[]{:S(2)}) collective-permute-start(bf16[448,1024]{1,0:T(8,128)(2,1)S(1)} %fusion.48), channel_id=1, source_target_pairs={{0,1},{1,0},{2,3},{3,2},{4,5},{5,4},{6,7},{7,6},{8,9},{9,8},{10,11... | collective-permute-start | bytes 2752520 | tf_op jit(solution)/shard_map/ppermute | solution.py:25
  243.6 63.8 %collective-permute-start.20 = (bf16[448,1024]{1,0:T(8,128)(2,1)S(1)}, bf16[448,1024]{1,0:T(8,128)(2,1)S(1)}, u32[]{:S(2)}, u32[]{:S(2)}) collective-permute-start(bf16[448,1024]{1,0:T(8,128)(2,1)S(1)} %fusion.45), channel_id=1, source_target_pairs={{0,1},{1,0},{2,3},{3,2},{4,5},{5,4},{6,7},{7,6},{8,9},{9,8},{10,11... | collective-permute-start | bytes 2752520 | tf_op jit(solution)/shard_map/ppermute | solution.py:25
  245.6 91.3 %collective-permute-start.17 = (bf16[448,1024]{1,0:T(8,128)(2,1)S(1)}, bf16[448,1024]{1,0:T(8,128)(2,1)S(1)}, u32[]{:S(2)}, u32[]{:S(2)}) collective-permute-start(bf16[448,1024]{1,0:T(8,128)(2,1)S(1)} %fusion.42), channel_id=1, source_target_pairs={{0,1},{1,0},{2,3},{3,2},{4,5},{5,4},{6,7},{7,6},{8,9},{9,8},{10,11... | collective-permute-start | bytes 2752520 | tf_op jit(solution)/shard_map/ppermute | solution.py:25
  263.1 98.8 %collective-permute-start.14 = (bf16[448,1024]{1,0:T(8,128)(2,1)S(1)}, bf16[448,1024]{1,0:T(8,128)(2,1)S(1)}, u32[]{:S(2)}, u32[]{:S(2)}) collective-permute-start(bf16[448,1024]{1,0:T(8,128)(2,1)S(1)} %fusion.39), channel_id=1, source_target_pairs={{0,1},{1,0},{2,3},{3,2},{4,5},{5,4},{6,7},{7,6},{8,9},{9,8},{10,11... | collective-permute-start | bytes 2752520 | tf_op jit(solution)/shard_map/ppermute | solution.py:25
  282.8 97.8 %collective-permute-start.11 = (bf16[448,1024]{1,0:T(8,128)(2,1)S(1)}, bf16[448,1024]{1,0:T(8,128)(2,1)S(1)}, u32[]{:S(2)}, u32[]{:S(2)}) collective-permute-start(bf16[448,1024]{1,0:T(8,128)(2,1)S(1)} %fusion.36), channel_id=1, source_target_pairs={{0,1},{1,0},{2,3},{3,2},{4,5},{5,4},{6,7},{7,6},{8,9},{9,8},{10,11... | collective-permute-start | bytes 2752520 | tf_op jit(solution)/shard_map/ppermute | solution.py:25
  307.4 76.9 %collective-permute-start.27 = (bf16[224,1024]{1,0:T(8,128)(2,1)S(1)}, bf16[224,1024]{1,0:T(8,128)(2,1)S(1)}, u32[]{:S(2)}, u32[]{:S(2)}) collective-permute-start(bf16[224,1024]{1,0:T(8,128)(2,1)S(1)} %slice.324), channel_id=1, source_target_pairs={{0,2},{1,3},{2,0},{3,1},{4,6},{5,7},{6,4},{7,5},{8,10},{9,11},{10,... | collective-permute-start | bytes 1376264 | tf_op jit(solution)/shard_map/ppermute | solution.py:25
  336.9 50.6 %collective-permute-start.24 = (bf16[224,1024]{1,0:T(8,128)(2,1)S(1)}, bf16[224,1024]{1,0:T(8,128)(2,1)S(1)}, u32[]{:S(2)}, u32[]{:S(2)}) collective-permute-start(bf16[224,1024]{1,0:T(8,128)(2,1)S(1)} %slice.325), channel_id=1, source_target_pairs={{0,2},{1,3},{2,0},{3,1},{4,6},{5,7},{6,4},{7,5},{8,10},{9,11},{10,... | collective-permute-start | bytes 1376264 | tf_op jit(solution)/shard_map/ppermute | solution.py:25
  362.0 68.6 %collective-permute-start.21 = (bf16[224,1024]{1,0:T(8,128)(2,1)S(1)}, bf16[224,1024]{1,0:T(8,128)(2,1)S(1)}, u32[]{:S(2)}, u32[]{:S(2)}) collective-permute-start(bf16[224,1024]{1,0:T(8,128)(2,1)S(1)} %slice.326), channel_id=1, source_target_pairs={{0,2},{1,3},{2,0},{3,1},{4,6},{5,7},{6,4},{7,5},{8,10},{9,11},{10,... | collective-permute-start | bytes 1376264 | tf_op jit(solution)/shard_map/ppermute | solution.py:25
  380.6 79.7 %collective-permute-start.18 = (bf16[224,1024]{1,0:T(8,128)(2,1)S(1)}, bf16[224,1024]{1,0:T(8,128)(2,1)S(1)}, u32[]{:S(2)}, u32[]{:S(2)}) collective-permute-start(bf16[224,1024]{1,0:T(8,128)(2,1)S(1)} %slice.327), channel_id=1, source_target_pairs={{0,2},{1,3},{2,0},{3,1},{4,6},{5,7},{6,4},{7,5},{8,10},{9,11},{10,... | collective-permute-start | bytes 1376264 | tf_op jit(solution)/shard_map/ppermute | solution.py:25
  384.3 74.2 %collective-permute-start.15 = (bf16[224,1024]{1,0:T(8,128)(2,1)S(1)}, bf16[224,1024]{1,0:T(8,128)(2,1)S(1)}, u32[]{:S(2)}, u32[]{:S(2)}) collective-permute-start(bf16[224,1024]{1,0:T(8,128)(2,1)S(1)} %slice.328), channel_id=1, source_target_pairs={{0,2},{1,3},{2,0},{3,1},{4,6},{5,7},{6,4},{7,5},{8,10},{9,11},{10,... | collective-permute-start | bytes 1376264 | tf_op jit(solution)/shard_map/ppermute | solution.py:25
  387.4 70.9 %collective-permute-start.12 = (bf16[224,1024]{1,0:T(8,128)(2,1)S(1)}, bf16[224,1024]{1,0:T(8,128)(2,1)S(1)}, u32[]{:S(2)}, u32[]{:S(2)}) collective-permute-start(bf16[224,1024]{1,0:T(8,128)(2,1)S(1)} %slice.329), channel_id=1, source_target_pairs={{0,2},{1,3},{2,0},{3,1},{4,6},{5,7},{6,4},{7,5},{8,10},{9,11},{10,... | collective-permute-start | bytes 1376264 | tf_op jit(solution)/shard_map/ppermute | solution.py:25
  430.5 57.0 %collective-permute-start.28 = (bf16[224,1024]{1,0:T(8,128)(2,1)S(1)}, bf16[224,1024]{1,0:T(8,128)(2,1)S(1)}, u32[]{:S(2)}, u32[]{:S(2)}) collective-permute-start(bf16[224,1024]{1,0:T(8,128)(2,1)S(1)} %fusion.54), channel_id=1, source_target_pairs={{0,4},{4,8},{8,12},{12,16},{16,20},{20,24},{24,28},{28,0},{1,5},{5... | collective-permute-start | bytes 1376264 | tf_op jit(solution)/shard_map/ppermute | solution.py:30
  458.4 28.9 %collective-permute-start.25 = (bf16[224,1024]{1,0:T(8,128)(2,1)S(1)}, bf16[224,1024]{1,0:T(8,128)(2,1)S(1)}, u32[]{:S(2)}, u32[]{:S(2)}) collective-permute-start(bf16[224,1024]{1,0:T(8,128)(2,1)S(1)} %fusion.56), channel_id=1, source_target_pairs={{0,4},{4,8},{8,12},{12,16},{16,20},{20,24},{24,28},{28,0},{1,5},{5... | collective-permute-start | bytes 1376264 | tf_op jit(solution)/shard_map/ppermute | solution.py:30
  458.5 13.6 %collective-permute-start.13 = (bf16[224,1024]{1,0:T(8,128)(2,1)S(1)}, bf16[224,1024]{1,0:T(8,128)(2,1)S(1)}, u32[]{:S(2)}, u32[]{:S(2)}) collective-permute-start(bf16[224,1024]{1,0:T(8,128)(2,1)S(1)} %fusion.64), channel_id=1, source_target_pairs={{0,4},{4,8},{8,12},{12,16},{16,20},{20,24},{24,28},{28,0},{1,5},{5... | collective-permute-start | bytes 1376264 | tf_op jit(solution)/shard_map/ppermute | solution.py:30
  460.3 16.7 %collective-permute-start.16 = (bf16[224,1024]{1,0:T(8,128)(2,1)S(1)}, bf16[224,1024]{1,0:T(8,128)(2,1)S(1)}, u32[]{:S(2)}, u32[]{:S(2)}) collective-permute-start(bf16[224,1024]{1,0:T(8,128)(2,1)S(1)} %fusion.62), channel_id=1, source_target_pairs={{0,4},{4,8},{8,12},{12,16},{16,20},{20,24},{24,28},{28,0},{1,5},{5... | collective-permute-start | bytes 1376264 | tf_op jit(solution)/shard_map/ppermute | solution.py:30
  472.1 15.0 %collective-permute-start.22 = (bf16[224,1024]{1,0:T(8,128)(2,1)S(1)}, bf16[224,1024]{1,0:T(8,128)(2,1)S(1)}, u32[]{:S(2)}, u32[]{:S(2)}) collective-permute-start(bf16[224,1024]{1,0:T(8,128)(2,1)S(1)} %fusion.58), channel_id=1, source_target_pairs={{0,4},{4,8},{8,12},{12,16},{16,20},{20,24},{24,28},{28,0},{1,5},{5... | collective-permute-start | bytes 1376264 | tf_op jit(solution)/shard_map/ppermute | solution.py:30
  472.1 14.7 %collective-permute-start.19 = (bf16[224,1024]{1,0:T(8,128)(2,1)S(1)}, bf16[224,1024]{1,0:T(8,128)(2,1)S(1)}, u32[]{:S(2)}, u32[]{:S(2)}) collective-permute-start(bf16[224,1024]{1,0:T(8,128)(2,1)S(1)} %fusion.60), channel_id=1, source_target_pairs={{0,4},{4,8},{8,12},{12,16},{16,20},{20,24},{24,28},{28,0},{1,5},{5... | collective-permute-start | bytes 1376264 | tf_op jit(solution)/shard_map/ppermute | solution.py:30
  (14 other events, 174.9 us)

commit v2 on v1

v2 whole, which is shorter than its diff:
```python
import math

import jax
import jax.numpy as jnp
from jax import lax
from jax.experimental import pallas as pl
from jax.experimental.pallas import tpu as pltpu
from jax.sharding import PartitionSpec as P

HDIM = 128
SPAN = 448
NCHUNK = 40
SLOTS = 3
VIDS = 2
TOKS = 896
KEYS = 1344
PAIR = 2 * HDIM
FLOOR = -3.0e38
SCALE = HDIM ** (-0.5) * math.log2(math.e)
COLS = 512
LAG = 2


def swapped(shard, axis, bit):
    devices = lax.axis_size(axis)
    return lax.ppermute(shard, axis, [(i, i ^ bit) for i in range(devices)])


def passed_along(shard, axis, by):
    devices = lax.axis_size(axis)
    return lax.ppermute(shard, axis, [(i, (i + by) % devices) for i in range(devices)])


def visible_slots(span_id, filled, span_mask):
    row_mask = lax.dynamic_index_in_dim(span_mask, span_id, 0, keepdims=False)
    slot_ids = jnp.arange(SLOTS, dtype=jnp.int32)
    wanted = span_id - 1 - slot_ids
    columns = jnp.arange(NCHUNK, dtype=jnp.int32)
    looked = jnp.sum(jnp.where(columns[None, :] == wanted[:, None], row_mask[None, :], 0), axis=1)
    return (slot_ids < filled) & (looked == 1)


def dot_t(left, right):
    return lax.dot_general(left, right, (((1,), (1,)), ((), ())), preferred_element_type=jnp.float32)


def far_kernel(q_ref, k_ref, v_ref, bias_ref, acc_ref, high_ref, total_ref):
    for head in range(2):
        cols = slice(head * HDIM, (head + 1) * HDIM)
        scores = dot_t(q_ref[:, cols], k_ref[0, 0, 0, :, cols]) + bias_ref[0:1, :]
        highest = jnp.maximum(jnp.max(scores, axis=1, keepdims=True), FLOOR)
        raised = jnp.exp2(scores * SCALE - highest * SCALE)
        total = jnp.sum(raised, axis=1, keepdims=True)
        acc_ref[:, cols] = jnp.dot(
            raised.astype(jnp.bfloat16), v_ref[0, 0, 0, :, cols], preferred_element_type=jnp.float32
        )
        high_ref[:, cols] = jnp.broadcast_to(highest, (SPAN, HDIM))
        total_ref[:, cols] = jnp.broadcast_to(total, (SPAN, HDIM))


def near_kernel(q_ref, k_ref, v_ref, acc_ref, high_ref, total_ref, *rest):
    out_ref = rest[-1]
    for head in range(2):
        cols = slice(head * HDIM, (head + 1) * HDIM)
        scores = dot_t(q_ref[:, cols], k_ref[0, :, cols])
        far_high = high_ref[:, cols]
        near_high = jnp.broadcast_to(jnp.max(scores, axis=1, keepdims=True), (SPAN, HDIM))
        highest = jnp.maximum(near_high, far_high) * SCALE
        wide = jnp.concatenate([highest] * -(-SPAN // HDIM), axis=1)[:, :SPAN]
        raised = jnp.exp2(scores * SCALE - wide)
        fade = jnp.exp2(far_high * SCALE - highest)
        near_total = jnp.broadcast_to(jnp.sum(raised, axis=1, keepdims=True), (SPAN, HDIM))
        total = near_total + total_ref[:, cols] * fade
        mixed = jnp.dot(raised.astype(jnp.bfloat16), v_ref[0, :, cols], preferred_element_type=jnp.float32)
        mixed = (mixed + acc_ref[:, cols] * fade) / total
        out_ref[:, cols] = mixed.astype(jnp.bfloat16)


def far_mix(queries, cache_kv, live_slots):
    width = queries.shape[1]
    bias = jnp.where(jnp.repeat(live_slots, SPAN), 0.0, -jnp.inf).astype(jnp.float32)
    bias = jnp.broadcast_to(bias[None, :], (8, KEYS))
    block = pl.BlockSpec((SPAN, PAIR), lambda b, h: (b, h))
    return pl.pallas_call(
        far_kernel,
        grid=(VIDS, width // PAIR),
        in_specs=[
            block,
            pl.BlockSpec((1, 1, 1, KEYS, PAIR), lambda b, h: (0, 0, b, 0, h)),
            pl.BlockSpec((1, 1, 1, KEYS, PAIR), lambda b, h: (0, 1, b, 0, h)),
            pl.BlockSpec((8, KEYS), lambda b, h: (0, 0)),
        ],
        out_specs=[block] * 3,
        out_shape=[jax.ShapeDtypeStruct((TOKS, width), jnp.float32)] * 3,
        compiler_params=pltpu.CompilerParams(vmem_limit_bytes=40 * 1024 * 1024),
        cost_estimate=pl.CostEstimate(
            flops=4 * TOKS * KEYS * width * 4,
            bytes_accessed=2 * VIDS * KEYS * width * 2 + TOKS * width * 14,
            transcendentals=TOKS * KEYS * (width // HDIM),
        ),
    )(queries, cache_kv, cache_kv, bias)


def near_mix(queries, own_kv, far_parts, first, earlier):
    width, group = queries.shape[1], own_kv.shape[2]
    block = pl.BlockSpec((SPAN, PAIR), lambda b, h: (b, h + first))
    operands = [queries, own_kv, own_kv, *far_parts]
    in_specs = [
        block,
        pl.BlockSpec((1, SPAN, PAIR), lambda b, h: (0, b, h)),
        pl.BlockSpec((1, SPAN, PAIR), lambda b, h: (1, b, h)),
        block,
        block,
        block,
    ]
    aliases = {}
    if earlier is not None:
        aliases = {len(operands): 0}
        operands.append(earlier)
        in_specs.append(pl.BlockSpec(memory_space=pl.ANY))
    return pl.pallas_call(
        near_kernel,
        grid=(VIDS, group // PAIR),
        in_specs=in_specs,
        out_specs=block,
        out_shape=jax.ShapeDtypeStruct((TOKS, width), jnp.bfloat16),
        input_output_aliases=aliases,
        compiler_params=pltpu.CompilerParams(vmem_limit_bytes=40 * 1024 * 1024),
        cost_estimate=pl.CostEstimate(
            flops=4 * TOKS * SPAN * group * 4,
            bytes_accessed=TOKS * group * 20,
            transcendentals=TOKS * SPAN * (group // HDIM),
        ),
    )(*operands)


def flipped(place, bits):
    bit = 1
    while bit <= bits:
        if bits & bit:
            place = place + bit - 2 * bit * lax.rem(lax.div(place, bit), 2)
        bit *= 2
    return place


def sum_kernel(devices, heads_ref, proj_ref, out_ref, w_buf, acc, *rest):
    stages = devices.bit_length() - 1
    sends, lands = rest[: stages + 1], rest[stages + 1 : 2 * stages + 1]
    w_sem, send_sem, recv_sem = rest[2 * stages + 1 :]
    place, section = lax.axis_index("sp"), lax.axis_index("section")
    sections = lax.axis_size("section")
    after = lax.rem(section + 1, sections)
    before = lax.rem(section + sections - 1, sections)
    rows = heads_ref.shape[0] // devices
    chunks = acc.shape[0]
    cols = acc.shape[2]
    mesh_id = pl.DeviceIdType.MESH
    partners = [(section, flipped(place, 1 << k)) for k in range(stages)]

    barrier = pltpu.get_barrier_semaphore()
    for other in partners + [(before, place)]:
        pl.semaphore_signal(barrier, inc=1, device_id=other, device_id_type=mesh_id)
    pl.semaphore_wait(barrier, stages + 1)

    def columns(t):
        return pl.ds(pl.multiple_of(t * cols, cols), cols)

    def fetch(t):
        slot = lax.rem(t, 2)
        return pltpu.make_async_copy(proj_ref.at[0, :, columns(t)], w_buf.at[slot], w_sem.at[slot])

    def move(k, t):
        return pltpu.make_async_remote_copy(
            src_ref=sends[k].at[t],
            dst_ref=lands[k].at[t] if k < stages else out_ref.at[:, columns(t)],
            send_sem=send_sem.at[k, t],
            recv_sem=recv_sem.at[k, t],
            device_id=partners[k] if k < stages else (after, place),
            device_id_type=mesh_id,
        )

    def product(t, flips):
        start = pl.multiple_of(flipped(place, flips) * rows, 16)
        return jnp.dot(
            heads_ref[pl.ds(start, rows), :], w_buf[lax.rem(t, 2)], preferred_element_type=jnp.float32
        )

    def multiply(t):
        fetch(t).wait()

        @pl.when(t + 1 < chunks)
        def _():
            fetch(t + 1).start()

        for i in range(devices // 2):
            sends[0][t, i * rows : (i + 1) * rows] = product(t, 2 * i + 1).astype(jnp.bfloat16)
        move(0, t).start()
        for i in range(devices // 2):
            acc[t, i * rows : (i + 1) * rows] = product(t, 2 * i)

    def combine(k, t):
        move(k, t).wait_recv()
        count = devices >> (k + 1)
        for i in range(count):
            spot = i << k
            summed = acc[t, spot * rows : (spot + 1) * rows] + lands[k][
                t, i * rows : (i + 1) * rows
            ].astype(jnp.float32)
            if i % 2 or count == 1:
                j = i // 2
                sends[k + 1][t, j * rows : (j + 1) * rows] = summed.astype(jnp.bfloat16)
            else:
                acc[t, spot * rows : (spot + 1) * rows] = summed
        move(k + 1, t).start()

    fetch(0).start()

    def step(t, carry):
        @pl.when(t < chunks)
        def _():
            multiply(t)

        for k in range(stages):
            done = t - LAG * (k + 1)

            @pl.when((done >= 0) & (done < chunks))
            def _():
                combine(k, done)

        return carry

    lax.fori_loop(0, chunks + LAG * stages, step, 0)

    def finish(t, carry):
        move(stages, t).wait_recv()
        for k in range(stages + 1):
            move(k, t).wait_send()
        return carry

    lax.fori_loop(0, chunks, finish, 0)


def summed_and_moved(heads_all, out_proj, devices):
    width, model = out_proj.shape[1], out_proj.shape[2]
    rows = TOKS // devices
    chunks = model // COLS
    stages = devices.bit_length() - 1
    sizes = [max(devices >> (k + 1), 1) * rows for k in range(stages + 1)]
    return pl.pallas_call(
        lambda *refs: sum_kernel(devices, *refs),
        out_shape=jax.ShapeDtypeStruct((rows, model), jnp.bfloat16),
        in_specs=[pl.BlockSpec(memory_space=pltpu.VMEM), pl.BlockSpec(memory_space=pl.ANY)],
        out_specs=pl.BlockSpec(memory_space=pl.ANY),
        scratch_shapes=[
            pltpu.VMEM((2, width, COLS), jnp.bfloat16),
            pltpu.VMEM((chunks, sizes[0], COLS), jnp.float32),
        ]
        + [pltpu.VMEM((chunks, size, COLS), jnp.bfloat16) for size in sizes]
        + [pltpu.VMEM((chunks, size, COLS), jnp.bfloat16) for size in sizes[:-1]]
        + [
            pltpu.SemaphoreType.DMA((2,)),
            pltpu.SemaphoreType.DMA((stages + 1, chunks)),
            pltpu.SemaphoreType.DMA((stages + 1, chunks)),
        ],
        compiler_params=pltpu.CompilerParams(
            collective_id=0, has_side_effects=True, vmem_limit_bytes=58 * 1024 * 1024
        ),
        cost_estimate=pl.CostEstimate(
            flops=2 * TOKS * width * model, bytes_accessed=2 * width * model, transcendentals=0
        ),
    )(heads_all, out_proj)


def heads_gathered(cut, rows, place, devices):
    piece = cut(place)
    whole = jnp.zeros(piece.shape[:-2] + (rows * devices, piece.shape[-1]), piece.dtype)
    lead = (0,) * (piece.ndim - 2)
    for bit in range(devices):
        other = place ^ bit
        piece = cut(other)
        if bit:
            piece = swapped(piece, "sp", bit)
        whole = lax.dynamic_update_slice(whole, piece, (*lead, other * rows, 0))
    return whole


def per_device(resid, qkv, cache_kv, out_proj, gate, span_ids, cache_counts, span_mask):
    own_rows = resid.shape[1]
    width = cache_kv.shape[4]
    devices = lax.axis_size("sp")
    place = lax.axis_index("sp")
    live_slots = visible_slots(span_ids[0], cache_counts[0], span_mask)

    def cut_queries(other):
        return lax.dynamic_slice(qkv[0, :, 0], (0, other * width), (own_rows, width))

    queries = heads_gathered(cut_queries, own_rows, place, devices)
    far_parts = far_mix(queries, cache_kv, live_slots)

    pairs = width // PAIR
    front = (pairs + 1) // 2
    heads_all = None
    for first, count in ((0, front), (front, pairs - front)):

        def cut_kv(other):
            begin = (0, other * width + first * PAIR)
            size = (own_rows, count * PAIR)
            return jnp.stack([lax.dynamic_slice(qkv[0, :, i], begin, size) for i in (1, 2)])

        own_kv = heads_gathered(cut_kv, own_rows, place, devices)
        heads_all = near_mix(queries, own_kv, far_parts, first, heads_all)

    resid_prev = passed_along(resid[0], "section", 1)
    gate_prev = passed_along(gate[0], "section", 1)
    moved = summed_and_moved(heads_all, out_proj, devices).astype(jnp.float32)
    video_of = (place * own_rows + jnp.arange(own_rows, dtype=jnp.int32)) // SPAN
    gains = jnp.where((video_of == 0)[:, None], gate_prev[0:1], gate_prev[1:2])
    return (resid_prev + gains * moved)[None]


def solution(mesh):
    in_specs = (
        P("section", "sp", None),
        P("section", "sp", None, None),
        P("section", None, None, None, "sp"),
        P("section", "sp", None),
        P("section", None, None),
        P("section"),
        P("section"),
        P(),
    )
    out_specs = P("section", "sp", None)
    return jax.shard_map(
        per_device, mesh=mesh, in_specs=in_specs, out_specs=out_specs, check_vma=False
    )
```

time: 491 us -> 451 us (0.919)
  Pallas kernels: 69.8 us -> 259 us
  waiting for transfers between devices: 292 us -> 130 us
  matrix products: 37.7 us -> 0 us
  starting transfers between devices: 56.3 us -> 19.6 us
  other arithmetic: 2.1 us -> 13.1 us
    pallas_call x1 -> x3, Pallas kernels: 36.8 us -> 225 us  [the longest x1 208 us: summed_and_moved(): pl.pallas_call(lambda *refs: sum_kernel(devices, *refs), out_shape=jax.Sh...]
    ppermute x21 -> x9, waiting for transfers between devices: 267 us -> 130 us  [swapped(): return lax.ppermute(shard, axis, [(i, i ^ bit) for i in range(devices)])]
    dot_general x12 -> x0, matrix products: 37.7 us -> none  [the longest x6 21.3 us: per_device(): summed = jnp.dot(even, proj, preferred_element_type=jnp.float32)]
    ppermute x21 -> x9, starting transfers between devices: 53.8 us -> 19.6 us  [swapped(): return lax.ppermute(shard, axis, [(i, i ^ bit) for i in range(devices)])]
    ppermute x8 -> x2, waiting for transfers between devices: 25.2 us -> 0.01 us  [passed_along(): lax.ppermute(shard, axis, [(i, (i + by) % devices) for i in range(devices)])]
    broadcast_in_dim x0 -> x1, other arithmetic: none -> 7.05 us  [per_device(): return (resid_prev + gains * moved)[None]]
    dynamic_slice x4 -> x1, local copies, waits for them, and re-layouts: 8.18 us -> 1.24 us  [cut_queries(): lax.dynamic_slice(qkv[0, :, 0], (0, other * width), (own_rows, width))]
    another operation x0 -> x6, other arithmetic: none -> 5.7 us  [cut_kv(): jnp.stack([lax.dynamic_slice(qkv[0, :, i], begin, size) for i in (1, 2)])]
  transfers between devices with their start and end apart: 29 -> 11, of which waited for: 14 -> 4; matrix products, arithmetic and copies ran while one was open for 11% -> 4% of each run, Pallas kernels for 14% -> 57%
where the time goes in v2:
time: 451 us; the launch traced here: 450 us
  Pallas kernels  259 us (57%)
  waiting for transfers between devices  130 us (29%)
  local copies, waits for them, and re-layouts  28.1 us (6%)
  starting transfers between devices  19.6 us (4%)
  other arithmetic  13.1 us (3%)
    pallas_call x1, Pallas kernels, summed_and_moved(): pl.pallas_call(lambda *refs: sum_kernel(devices, *refs), out_shape=jax.Sh...  208 us
    ppermute x9, waiting for transfers between devices, swapped(): return lax.ppermute(shard, axis, [(i, i ^ bit) for i in range(devices)])  130 us
    pallas_call x1, Pallas kernels, far_mix(): pl.pallas_call(far_kernel, grid=(VIDS, width // PAIR), in_specs=[block, p...  33.7 us
    ppermute x9, starting transfers between devices, swapped(): return lax.ppermute(shard, axis, [(i, i ^ bit) for i in range(devices)])  19.6 us
    pallas_call x2, Pallas kernels, near_mix(): pl.pallas_call(near_kernel, grid=(VIDS, group // PAIR), in_specs=in_specs...  17 us
    dynamic_update_slice x10, local copies, waits for them, and re-layouts, heads_gathered(): whole = lax.dynamic_update_slice(whole, piece, (*lead, other * rows, 0))  10.1 us
  transfers between devices with their start and end apart: 11, of which 4 were waited for; matrix products, arithmetic and copies ran while one was open for 4% of the time, Pallas kernels for 57%

profile of v2, /device:TPU:0, one launch (start us, length us, event | category | flops | bytes accessed | tf_op | source)
XLA Modules:
  0.0 450.4 jit_solution(18287974177849830626)
XLA Ops:
  0.0 5.4 %fusion.2 = (bf16[1,224,1,6144]{3,1,2,0:T(8,128)(2,1)S(1)}, bf16[1,224,1,6144]{3,1,2,0:T(8,128)(2,1)}, bf16[1,224,1,6144]{3,1,2,0:T(8,128)(2,1)}) fusion(bf16[1,224,3,6144]{3,1,2,0:T(8,128)(2,1)} %param.9), kind=kLoop, calls=%fused_computation.46 | loop fusion | bytes 16515072 | tf_op jit(solution)/shard_map/slice | solution.py:308
  5.4 3.3 dynamic-slice_bitcast_fusion.3
  8.7 0.9 pad_maximum_fusion.3
  9.6 3.0 collective-permute-start.8
  12.7 1.0 pad_maximum_fusion.4
  13.7 2.6 collective-permute-start.9
  16.2 0.9 pad_maximum_fusion.5
  20.6 0.9 pad_maximum_fusion.1
  21.5 1.0 pad_maximum_fusion.2
  23.2 1.0 copy-done.2
  24.3 2.3 copy-done.8
  26.6 1.2 dynamic-slice_bitcast_fusion
  28.0 3.5 collective-permute-start.6
  31.6 11.2 %collective-permute-done.8 = bf16[2,224,768]{2,1,0:T(8,128)(2,1)} collective-permute-done((bf16[2,224,768]{2,1,0:T(8,128)(2,1)}, bf16[2,224,768]{2,1,0:T(8,128)(2,1)}, u32[]{:S(2)}, u32[]{:S(2)}) %collective-permute-start.8) | collective-permute-done | bytes 688160 | tf_op jit(solution)/shard_map/ppermute | solution.py:26
  42.7 3.3 collective-permute-start.7
  46.1 27.1 %collective-permute-done.5 = bf16[2,224,768]{2,1,0:T(8,128)(2,1)} collective-permute-done((bf16[2,224,768]{2,1,0:T(8,128)(2,1)}, bf16[2,224,768]{2,1,0:T(8,128)(2,1)}, u32[]{:S(2)}, u32[]{:S(2)}) %collective-permute-start.5) | collective-permute-done | bytes 688160 | tf_op jit(solution)/shard_map/ppermute | solution.py:26
  73.1 2.5 collective-permute-start.2
  75.6 2.0 constant_dynamic-update-slice_fusion.1
  77.6 2.0 constant_dynamic-update-slice_fusion.4
  79.7 1.3 collective-permute-start.3
  81.0 2.0 constant_dynamic-update-slice_fusion
  83.0 53.4 %collective-permute-done.6 = bf16[2,224,768]{2,1,0:T(8,128)(2,1)S(1)} collective-permute-done((bf16[2,224,768]{2,1,0:T(8,128)(2,1)}, bf16[2,224,768]{2,1,0:T(8,128)(2,1)S(1)}, u32[]{:S(2)}, u32[]{:S(2)}) %collective-permute-start.6) | collective-permute-done | bytes 688160 | tf_op jit(solution)/shard_map/ppermute | solution.py:26
  136.4 2.5 collective-permute-start.4
  139.8 2.0 constant_dynamic-update-slice_fusion.8.k_ref.v_ref
  142.8 37.9 %collective-permute-done.3 = bf16[224,1536]{1,0:T(8,128)(2,1)S(1)} collective-permute-done((bf16[224,1536]{1,0:T(8,128)(2,1)S(1)}, bf16[224,1536]{1,0:T(8,128)(2,1)S(1)}, u32[]{:S(2)}, u32[]{:S(2)}) %collective-permute-start.3) | collective-permute-done | bytes 688160 | tf_op jit(solution)/shard_map/ppermute | solution.py:26
  180.8 33.7 %shard_map.82 = (f32[896,1536]{1,0:T(8,128)S(1)}, f32[896,1536]{1,0:T(8,128)S(1)}, f32[896,1536]{1,0:T(8,128)}) custom-call(bf16[896,1536]{1,0:T(8,128)(2,1)S(1)} %constant_dynamic-update-slice_fusion.5.q_ref, bf16[1,2,2,1344,1536]{4,3,2,1,0:T(8,128)(2,1)} %v_ref.1, bf16[1,2,2,1344,1536]{4,3,2,1,0:T(8,128)(2,1)} %v_ref.1, ...), custom_call_target="tpu_custom_call" | custom-call | flops 29595009024 | bytes 35782656 | tf_op jit(solution)/shard_map/pallas_call | solution.py:84
  214.5 2.5 copy-done.6
  217.0 8.5 %shard_map.83.rest_0_ = bf16[896,1536]{1,0:T(8,128)(2,1)S(1)} custom-call(bf16[896,1536]{1,0:T(8,128)(2,1)S(1)} %constant_dynamic-update-slice_fusion.5.q_ref, bf16[2,896,768]{2,1,0:T(8,128)(2,1)S(1)} %copy-done.3, bf16[2,896,768]{2,1,0:T(8,128)(2,1)S(1)} %copy-done.3, f32[896,1536]{1,0:T(8,128)S(1)} %get-tuple-element.8.acc_ref, f32[896,1536]{1,0:T(8,128)} %copy-done.6, ...), custom_call_target="tpu_custom_call" | custom-call | flops 4932501504 | bytes 13762560 | tf_op jit(solution)/shard_map/pallas_call | solution.py:121
  225.5 8.4 %shard_map.84.refs_0_ = bf16[896,1536]{1,0:T(8,128)(2,1)S(1)} custom-call(bf16[896,1536]{1,0:T(8,128)(2,1)S(1)} %constant_dynamic-update-slice_fusion.5.q_ref, bf16[2,896,768]{2,1,0:T(8,128)(2,1)S(1)} %copy-done.5, bf16[2,896,768]{2,1,0:T(8,128)(2,1)S(1)} %copy-done.5, f32[896,1536]{1,0:T(8,128)S(1)} %get-tuple-element.8.acc_ref, ...), custom_call_target="tpu_custom_call", output_to_operand_aliasing={{}: (6, {})} | custom-call | flops 4932501504 | bytes 13762560 | tf_op jit(solution)/shard_map/pallas_call | solution.py:121
  234.0 1.5 copy-done.7
  235.5 207.8 %shard_map.85 = bf16[224,6144]{1,0:T(8,128)(2,1)} custom-call(bf16[896,1536]{1,0:T(8,128)(2,1)} %copy-done.7, bf16[1,1536,6144]{2,1,0:T(8,128)(2,1)} %refs_1_.1), custom_call_target="tpu_custom_call" | custom-call | flops 16911433728 | bytes 18874368 | tf_op jit(solution)/shard_map/pallas_call | solution.py:249
  443.4 7.1 %add_bitcast_fusion = f32[1,224,6144]{2,1,0:T(8,128)} fusion(f32[224,6144]{1,0:T(8,128)} %collective-permute-done, bf16[224,6144]{1,0:T(8,128)(2,1)} %shard_map.85, f32[6144]{0:T(1024)S(1)} %bitcast.56, f32[6144]{0:T(1024)S(1)} %bitcast.55, pred[224]{0:T(512)(128)(4,1)S(1)} %fusion), kind=kLoop, calls=%fused_computation | loop fusion | flops 5505024 | bytes 13811936 | tf_op jit(solution)/shard_map/broadcast_in_dim | solution.py:318
  (60 shorter events, 5.0 us)
Async XLA Ops:
  0.0 20.3 %copy-start = (s32[40,40]{1,0:T(8,128)S(1)}, s32[40,40]{1,0:T(8,128)}, u32[]{:S(2)}) copy-start(s32[40,40]{1,0:T(8,128)} %param.15) | copy-start | bytes 19204
  8.7 11.8 %copy-start.13 = (bf16[1,224,768]{2,1,0:T(8,128)(2,1)S(1)}, bf16[1,224,768]{2,1,0:T(8,128)(2,1)}, u32[]{:S(2)}) copy-start(bf16[1,224,768]{2,1,0:T(8,128)(2,1)} %get-tuple-element.27) | copy-start | bytes 1032196
  8.7 11.8 %copy-start.14 = (bf16[1,224,768]{2,1,0:T(8,128)(2,1)S(1)}, bf16[1,224,768]{2,1,0:T(8,128)(2,1)}, u32[]{:S(2)}) copy-start(bf16[1,224,768]{2,1,0:T(8,128)(2,1)} %get-tuple-element.37) | copy-start | bytes 1032196
  9.6 33.1 %collective-permute-start.8 = (bf16[2,224,768]{2,1,0:T(8,128)(2,1)}, bf16[2,224,768]{2,1,0:T(8,128)(2,1)}, u32[]{:S(2)}, u32[]{:S(2)}) collective-permute-start(bf16[2,224,768]{2,1,0:T(8,128)(2,1)} %pad_maximum_fusion.3), channel_id=1, source_target_pairs={{0,1},{1,0},{2,3},{3,2},{4,5},{5,4},{6,7},{7,6},{8,9},{9,8},{10,11... | collective-permute-start | bytes 2064392 | tf_op jit(solution)/shard_map/ppermute | solution.py:26
  12.7 8.8 %copy-start.11 = (bf16[1,224,768]{2,1,0:T(8,128)(2,1)S(1)}, bf16[1,224,768]{2,1,0:T(8,128)(2,1)}, u32[]{:S(2)}) copy-start(bf16[1,224,768]{2,1,0:T(8,128)(2,1)} %get-tuple-element.26) | copy-start | bytes 1032196
  12.7 8.8 %copy-start.12 = (bf16[1,224,768]{2,1,0:T(8,128)(2,1)S(1)}, bf16[1,224,768]{2,1,0:T(8,128)(2,1)}, u32[]{:S(2)}) copy-start(bf16[1,224,768]{2,1,0:T(8,128)(2,1)} %get-tuple-element.38) | copy-start | bytes 1032196
  13.7 66.0 %collective-permute-start.9 = (bf16[2,224,768]{2,1,0:T(8,128)(2,1)}, bf16[2,224,768]{2,1,0:T(8,128)(2,1)}, u32[]{:S(2)}, u32[]{:S(2)}) collective-permute-start(bf16[2,224,768]{2,1,0:T(8,128)(2,1)} %pad_maximum_fusion.4), channel_id=1, source_target_pairs={{0,2},{1,3},{2,0},{3,1},{4,6},{5,7},{6,4},{7,5},{8,10},{9,11},{10,... | collective-permute-start | bytes 2064392 | tf_op jit(solution)/shard_map/ppermute | solution.py:26
  17.2 122.6 %collective-permute-start.10 = (bf16[2,224,768]{2,1,0:T(8,128)(2,1)}, bf16[2,224,768]{2,1,0:T(8,128)(2,1)}, u32[]{:S(2)}, u32[]{:S(2)}) collective-permute-start(bf16[2,224,768]{2,1,0:T(8,128)(2,1)} %pad_maximum_fusion.5), channel_id=1, source_target_pairs={{0,3},{1,2},{2,1},{3,0},{4,7},{5,6},{6,5},{7,4},{8,11},{9,10},{10,... | collective-permute-start | bytes 2064392 | tf_op jit(solution)/shard_map/ppermute | solution.py:26
  18.1 55.1 %collective-permute-start.5 = (bf16[2,224,768]{2,1,0:T(8,128)(2,1)}, bf16[2,224,768]{2,1,0:T(8,128)(2,1)}, u32[]{:S(2)}, u32[]{:S(2)}) collective-permute-start(bf16[2,224,768]{2,1,0:T(8,128)(2,1)} %pad_maximum_fusion), channel_id=1, source_target_pairs={{0,1},{1,0},{2,3},{3,2},{4,5},{5,4},{6,7},{7,6},{8,9},{9,8},{10,11... | collective-permute-start | bytes 2064392 | tf_op jit(solution)/shard_map/ppermute | solution.py:26
  19.0 9.1 %collective-permute-start.1 = (f32[2,6144]{1,0:T(2,128)}, f32[2,6144]{1,0:T(2,128)S(1)}, u32[]{:S(2)}, u32[]{:S(2)}) collective-permute-start(f32[2,6144]{1,0:T(2,128)} %bitcast.1), channel_id=1, source_target_pairs={{0,4},{4,8},{8,12},{12,16},{16,20},{20,24},{24,28},{28,0},{1,5},{5... | collective-permute-start | bytes 147464 | tf_op jit(solution)/shard_map/ppermute | solution.py:31
  20.5 2.2 copy-start.9
  20.5 2.2 copy-start.10
  22.8 1.5 copy-start.2
  23.0 3.6 copy-start.8
  23.0 4.8 %copy-start.4 = (bf16[2,896,768]{2,1,0:T(8,128)(2,1)}, bf16[2,896,768]{2,1,0:T(8,128)(2,1)S(1)}, u32[]{:S(2)}) copy-start(bf16[2,896,768]{2,1,0:T(8,128)(2,1)S(1)} %maximum_dynamic-update-slice_fusion) | copy-start | bytes 8257540
  28.0 51.6 %copy-start.15 = (bf16[224,1536]{1,0:T(8,128)(2,1)S(1)}, bf16[224,1536]{1,0:T(8,128)(2,1)}, u32[]{:S(2)}) copy-start(bf16[224,1536]{1,0:T(8,128)(2,1)} %get-tuple-element.31) | copy-start | bytes 2064388
  28.0 108.4 %collective-permute-start.6 = (bf16[2,224,768]{2,1,0:T(8,128)(2,1)}, bf16[2,224,768]{2,1,0:T(8,128)(2,1)S(1)}, u32[]{:S(2)}, u32[]{:S(2)}) collective-permute-start(bf16[2,224,768]{2,1,0:T(8,128)(2,1)} %pad_maximum_fusion.1), channel_id=1, source_target_pairs={{0,2},{1,3},{2,0},{3,1},{4,6},{5,7},{6,4},{7,5},{8,10},{9,11},{10,... | collective-permute-start | bytes 2064392 | tf_op jit(solution)/shard_map/ppermute | solution.py:26
  42.7 99.1 %collective-permute-start.7 = (bf16[2,224,768]{2,1,0:T(8,128)(2,1)}, bf16[2,224,768]{2,1,0:T(8,128)(2,1)S(1)}, u32[]{:S(2)}, u32[]{:S(2)}) collective-permute-start(bf16[2,224,768]{2,1,0:T(8,128)(2,1)} %pad_maximum_fusion.2), channel_id=1, source_target_pairs={{0,3},{1,2},{2,1},{3,0},{4,7},{5,6},{6,5},{7,4},{8,11},{9,10},{10,... | collective-permute-start | bytes 2064392 | tf_op jit(solution)/shard_map/ppermute | solution.py:26
  73.1 69.6 %collective-permute-start.2 = (bf16[224,1536]{1,0:T(8,128)(2,1)}, bf16[224,1536]{1,0:T(8,128)(2,1)S(1)}, u32[]{:S(2)}, u32[]{:S(2)}) collective-permute-start(bf16[224,1536]{1,0:T(8,128)(2,1)} %get-tuple-element.32), channel_id=1, source_target_pairs={{0,1},{1,0},{2,3},{3,2},{4,5},{5,4},{6,7},{7,6},{8,9},{9,8},{10,11... | collective-permute-start | bytes 2064392 | tf_op jit(solution)/shard_map/ppermute | solution.py:26
  79.7 101.0 %collective-permute-start.3 = (bf16[224,1536]{1,0:T(8,128)(2,1)S(1)}, bf16[224,1536]{1,0:T(8,128)(2,1)S(1)}, u32[]{:S(2)}, u32[]{:S(2)}) collective-permute-start(bf16[224,1536]{1,0:T(8,128)(2,1)S(1)} %copy-done.15), channel_id=1, source_target_pairs={{0,2},{1,3},{2,0},{3,1},{4,6},{5,7},{6,4},{7,5},{8,10},{9,11},{10,... | collective-permute-start | bytes 2064392 | tf_op jit(solution)/shard_map/ppermute | solution.py:26
  136.4 44.3 %collective-permute-start.4 = (bf16[224,1536]{1,0:T(8,128)(2,1)S(1)}, bf16[224,1536]{1,0:T(8,128)(2,1)S(1)}, u32[]{:S(2)}, u32[]{:S(2)}) collective-permute-start(bf16[224,1536]{1,0:T(8,128)(2,1)S(1)} %get-tuple-element.30), channel_id=1, source_target_pairs={{0,3},{1,2},{2,1},{3,0},{4,7},{5,6},{6,5},{7,4},{8,11},{9,10},{10,... | collective-permute-start | bytes 2064392 | tf_op jit(solution)/shard_map/ppermute | solution.py:26
  139.8 303.6 %collective-permute-start = (f32[224,6144]{1,0:T(8,128)}, f32[224,6144]{1,0:T(8,128)}, u32[]{:S(2)}, u32[]{:S(2)}) collective-permute-start(f32[224,6144]{1,0:T(8,128)} %bitcast.57), channel_id=1, source_target_pairs={{0,4},{4,8},{8,12},{12,16},{16,20},{20,24},{24,28},{28,0},{1,5},{5... | collective-permute-start | bytes 16515080 | tf_op jit(solution)/shard_map/ppermute | solution.py:31
  180.8 36.2 %copy-start.3 = (bf16[2,896,768]{2,1,0:T(8,128)(2,1)S(1)}, bf16[2,896,768]{2,1,0:T(8,128)(2,1)}, u32[]{:S(2)}) copy-start(bf16[2,896,768]{2,1,0:T(8,128)(2,1)} %constant_dynamic-update-slice_fusion.8.k_ref.v_ref) | copy-start | bytes 8257540
  214.5 2.5 copy-start.6
  217.0 8.6 %copy-start.5 = (bf16[2,896,768]{2,1,0:T(8,128)(2,1)S(1)}, bf16[2,896,768]{2,1,0:T(8,128)(2,1)}, u32[]{:S(2)}) copy-start(bf16[2,896,768]{2,1,0:T(8,128)(2,1)} %constant_dynamic-update-slice_fusion.2.k_ref.v_ref) | copy-start | bytes 8257540
  234.0 1.5 copy-start.7
  443.4 7.1 %copy-start.1 = (s32[40,40]{1,0:T(8,128)S(1)}, s32[40,40]{1,0:T(8,128)}, u32[]{:S(2)}) copy-start(s32[40,40]{1,0:T(8,128)} %param.15) | copy-start | bytes 19204

commit v3 on v2

--- a/solution.py
+++ b/solution.py
@@ -17,8 +17,8 @@
 PAIR = 2 * HDIM
 FLOOR = -3.0e38
 SCALE = HDIM ** (-0.5) * math.log2(math.e)
-COLS = 512
-LAG = 2
+COLS = 256
+LAG = 3
 
 
 def swapped(shard, axis, bit):
@@ -94,9 +94,9 @@
         out_shape=[jax.ShapeDtypeStruct((TOKS, width), jnp.float32)] * 3,
         compiler_params=pltpu.CompilerParams(vmem_limit_bytes=40 * 1024 * 1024),
         cost_estimate=pl.CostEstimate(
-            flops=4 * TOKS * KEYS * width * 4,
-            bytes_accessed=2 * VIDS * KEYS * width * 2 + TOKS * width * 14,
-            transcendentals=TOKS * KEYS * (width // HDIM),
+            flops=4 * TOKS * KEYS * width,
+            bytes_accessed=TOKS * width,
+            transcendentals=0,
         ),
     )(queries, cache_kv, cache_kv, bias)
 
@@ -127,9 +127,9 @@
         input_output_aliases=aliases,
         compiler_params=pltpu.CompilerParams(vmem_limit_bytes=40 * 1024 * 1024),
         cost_estimate=pl.CostEstimate(
-            flops=4 * TOKS * SPAN * group * 4,
-            bytes_accessed=TOKS * group * 20,
-            transcendentals=TOKS * SPAN * (group // HDIM),
+            flops=4 * TOKS * SPAN * group,
+            bytes_accessed=TOKS * group,
+            transcendentals=0,
         ),
     )(*operands)
 
@@ -157,6 +157,8 @@
     mesh_id = pl.DeviceIdType.MESH
     partners = [(section, flipped(place, 1 << k)) for k in range(stages)]
 
+    first_fetch = pltpu.make_async_copy(proj_ref.at[0, :, pl.ds(0, cols)], w_buf.at[0], w_sem.at[0])
+    first_fetch.start()
     barrier = pltpu.get_barrier_semaphore()
     for other in partners + [(before, place)]:
         pl.semaphore_signal(barrier, inc=1, device_id=other, device_id_type=mesh_id)
@@ -212,8 +214,6 @@
             else:
                 acc[t, spot * rows : (spot + 1) * rows] = summed
         move(k + 1, t).start()
-
-    fetch(0).start()
 
     def step(t, carry):
         @pl.when(t < chunks)
@@ -275,13 +275,16 @@
     piece = cut(place)
     whole = jnp.zeros(piece.shape[:-2] + (rows * devices, piece.shape[-1]), piece.dtype)
     lead = (0,) * (piece.ndim - 2)
+    near_piece = piece
     for bit in range(devices):
         other = place ^ bit
         piece = cut(other)
         if bit:
             piece = swapped(piece, "sp", bit)
+        if bit == 1:
+            near_piece = piece
         whole = lax.dynamic_update_slice(whole, piece, (*lead, other * rows, 0))
-    return whole
+    return whole, near_piece
 
 
 def per_device(resid, qkv, cache_kv, out_proj, gate, span_ids, cache_counts, span_mask):
@@ -294,20 +297,21 @@
     def cut_queries(other):
         return lax.dynamic_slice(qkv[0, :, 0], (0, other * width), (own_rows, width))
 
-    queries = heads_gathered(cut_queries, own_rows, place, devices)
+    queries, near_piece = heads_gathered(cut_queries, own_rows, place, devices)
     far_parts = far_mix(queries, cache_kv, live_slots)
 
     pairs = width // PAIR
     front = (pairs + 1) // 2
     heads_all = None
-    for first, count in ((0, front), (front, pairs - front)):
+    for first, count, awaited in ((0, front, near_piece), (front, pairs - front, queries)):
+        source, _ = lax.optimization_barrier((qkv, awaited))
 
         def cut_kv(other):
             begin = (0, other * width + first * PAIR)
             size = (own_rows, count * PAIR)
-            return jnp.stack([lax.dynamic_slice(qkv[0, :, i], begin, size) for i in (1, 2)])
-
-        own_kv = heads_gathered(cut_kv, own_rows, place, devices)
+            return jnp.stack([lax.dynamic_slice(source[0, :, i], begin, size) for i in (1, 2)])
+
+        own_kv, _ = heads_gathered(cut_kv, own_rows, place, devices)
         heads_all = near_mix(queries, own_kv, far_parts, first, heads_all)
 
     resid_prev = passed_along(resid[0], "section", 1)

time: 451 us -> 400 us (0.89)
  waiting for transfers between devices: 130 us -> 55.7 us
  starting transfers between devices: 19.6 us -> 57.6 us
  Pallas kernels: 259 us -> 253 us
  other arithmetic: 13.1 us -> 7.76 us
  local copies, waits for them, and re-layouts: 28.1 us -> 23 us
    ppermute x9, waiting for transfers between devices: 130 us -> 55.7 us  [swapped(): return lax.ppermute(shard, axis, [(i, i ^ bit) for i in range(devices)])]
    ppermute x9, starting transfers between devices: 19.6 us -> 55.8 us  [swapped(): return lax.ppermute(shard, axis, [(i, i ^ bit) for i in range(devices)])]
    another operation x6, other arithmetic: 5.7 us -> 0.39 us  [cut_kv(): jnp.stack([lax.dynamic_slice(source[0, :, i], begin, size) for i in (1, 2)])]
    dynamic_update_slice x10, local copies, waits for them, and re-layouts: 10.1 us -> 4.92 us  [heads_gathered(): whole = lax.dynamic_update_slice(whole, piece, (*lead, other * rows, 0))]
    pallas_call x1, Pallas kernels: 208 us -> 203 us  [summed_and_moved(): pl.pallas_call(lambda *refs: sum_kernel(devices, *refs), out_shape=jax.Sh...]
  transfers between devices with their start and end apart: 11 -> 11, of which waited for: 4 -> 3; matrix products, arithmetic and copies ran while one was open for 4% -> 3% of each run, Pallas kernels for 57% -> 63%
where the time goes in v3:
time: 400 us; the launch traced here: 399 us
  Pallas kernels  253 us (63%)
  starting transfers between devices  57.6 us (14%)
  waiting for transfers between devices  55.7 us (14%)
  local copies, waits for them, and re-layouts  23 us (6%)
  other arithmetic  7.76 us (2%)
    pallas_call x1, Pallas kernels, summed_and_moved(): pl.pallas_call(lambda *refs: sum_kernel(devices, *refs), out_shape=jax.Sh...  203 us
    ppermute x9, starting transfers between devices, swapped(): return lax.ppermute(shard, axis, [(i, i ^ bit) for i in range(devices)])  55.8 us
    ppermute x9, waiting for transfers between devices, swapped(): return lax.ppermute(shard, axis, [(i, i ^ bit) for i in range(devices)])  55.7 us
    pallas_call x1, Pallas kernels, far_mix(): pl.pallas_call(far_kernel, grid=(VIDS, width // PAIR), in_specs=[block, p...  33.6 us
    pallas_call x2, Pallas kernels, near_mix(): pl.pallas_call(near_kernel, grid=(VIDS, group // PAIR), in_specs=in_specs...  16.8 us
  transfers between devices with their start and end apart: 11, of which 3 were waited for; matrix products, arithmetic and copies ran while one was open for 3% of the time, Pallas kernels for 63%

profile of v3, /device:TPU:0, one launch (start us, length us, event | category | flops | bytes accessed | tf_op | source)
XLA Modules:
  0.0 399.2 jit_solution(10307218207005734677)
XLA Ops:
  0.0 3.6 slice.16
  3.6 2.8 dynamic-slice_bitcast_fusion
  6.4 3.0 collective-permute-start.2
  9.4 2.6 collective-permute-start.3
  12.0 1.8 collective-permute-start
  15.2 0.2 select_reduce_fusion
  15.4 0.2 broadcast_in_dim.74
  15.6 1.2 bitcast_dynamic-update-slice_fusion
  17.0 22.2 %collective-permute-done.2 = bf16[224,1536]{1,0:T(8,128)(2,1)} collective-permute-done((bf16[224,1536]{1,0:T(8,128)(2,1)}, bf16[224,1536]{1,0:T(8,128)(2,1)}, u32[]{:S(2)}, u32[]{:S(2)}) %collective-permute-start.2) | collective-permute-done | bytes 688160 | tf_op jit(solution)/shard_map/ppermute | solution.py:26
  39.1 3.1 fusion.2
  42.3 0.3 dynamic-slice_bitcast_fusion.3
  42.8 3.8 collective-permute-start.9
  46.7 1.2 constant_dynamic-update-slice_fusion.7
  47.9 10.7 %collective-permute-done.3 = bf16[224,1536]{1,0:T(8,128)(2,1)} collective-permute-done((bf16[224,1536]{1,0:T(8,128)(2,1)}, bf16[224,1536]{1,0:T(8,128)(2,1)}, u32[]{:S(2)}, u32[]{:S(2)}) %collective-permute-start.3) | collective-permute-done | bytes 688160 | tf_op jit(solution)/shard_map/ppermute | solution.py:26
  58.5 2.5 collective-permute-start.10
  61.0 1.1 constant_dynamic-update-slice_fusion.6
  62.2 1.2 constant_dynamic-update-slice_fusion.5.q_ref
  63.3 0.6 fusion.3
  64.0 0.3 dynamic-slice_bitcast_fusion.11
  64.4 41.2 %collective-permute-start.5 = (bf16[2,224,768]{2,1,0:T(8,128)(2,1)S(1)}, bf16[2,224,768]{2,1,0:T(8,128)(2,1)S(1)}, u32[]{:S(2)}, u32[]{:S(2)}) collective-permute-start(bf16[2,224,768]{2,1,0:T(8,128)(2,1)S(1)} %pad_maximum_fusion), channel_id=1, source_target_pairs={{0,1},{1,0},{2,3},{3,2},{4,5},{5,4},{6,7},{7,6},{8,9},{9,8},{10,11... | collective-permute-start | bytes 2064392 | tf_op jit(solution)/shard_map/ppermute | solution.py:26
  105.6 33.6 %shard_map.82 = (f32[896,1536]{1,0:T(8,128)S(1)}, f32[896,1536]{1,0:T(8,128)S(1)}, f32[896,1536]{1,0:T(8,128)}) custom-call(bf16[896,1536]{1,0:T(8,128)(2,1)S(1)} %constant_dynamic-update-slice_fusion.5.q_ref, bf16[1,2,2,1344,1536]{4,3,2,1,0:T(8,128)(2,1)} %v_ref.1, bf16[1,2,2,1344,1536]{4,3,2,1,0:T(8,128)(2,1)} %v_ref.1, ...), custom_call_target="tpu_custom_call" | custom-call | flops 7398752256 | bytes 1376256 | tf_op jit(solution)/shard_map/pallas_call | solution.py:84
  139.2 2.5 copy-done.4
  141.8 0.2 broadcast.57.clone.1
  142.0 1.1 collective-permute-start.6
  143.4 1.5 collective-permute-start.7
  145.1 8.4 %shard_map.83.rest_0_ = bf16[896,1536]{1,0:T(8,128)(2,1)S(1)} custom-call(bf16[896,1536]{1,0:T(8,128)(2,1)S(1)} %constant_dynamic-update-slice_fusion.5.q_ref, bf16[2,896,768]{2,1,0:T(8,128)(2,1)S(1)} %constant_dynamic-update-slice_fusion.8.k_ref.v_ref, bf16[2,896,768]{2,1,0:T(8,128)(2,1)S(1)} %constant_dynamic-update-slice_fusion.8.k_ref.v_ref, ...), custom_call_target="tpu_custom_call" | custom-call | flops 1233125376 | bytes 688128 | tf_op jit(solution)/shard_map/pallas_call | solution.py:121
  153.6 22.8 %collective-permute-done.6 = bf16[2,224,768]{2,1,0:T(8,128)(2,1)S(1)} collective-permute-done((bf16[2,224,768]{2,1,0:T(8,128)(2,1)S(1)}, bf16[2,224,768]{2,1,0:T(8,128)(2,1)S(1)}, u32[]{:S(2)}, u32[]{:S(2)}) %collective-permute-start.6) | collective-permute-done | bytes 688160 | tf_op jit(solution)/shard_map/ppermute | solution.py:26
  176.6 2.6 copy-done.3
  179.1 8.4 %shard_map.84.refs_0_ = bf16[896,1536]{1,0:T(8,128)(2,1)S(1)} custom-call(bf16[896,1536]{1,0:T(8,128)(2,1)S(1)} %constant_dynamic-update-slice_fusion.5.q_ref, bf16[2,896,768]{2,1,0:T(8,128)(2,1)S(1)} %constant_dynamic-update-slice_fusion.2.k_ref.v_ref, ...), custom_call_target="tpu_custom_call", output_to_operand_aliasing={{}: (6, {})} | custom-call | flops 1233125376 | bytes 688128 | tf_op jit(solution)/shard_map/pallas_call | solution.py:121
  187.6 1.5 copy-done.5
  189.1 203.1 %shard_map.85 = bf16[224,6144]{1,0:T(8,128)(2,1)} custom-call(bf16[896,1536]{1,0:T(8,128)(2,1)} %copy-done.5, bf16[1,1536,6144]{2,1,0:T(8,128)(2,1)} %refs_1_.1), custom_call_target="tpu_custom_call" | custom-call | flops 16911433728 | bytes 18874368 | tf_op jit(solution)/shard_map/pallas_call | solution.py:249
  392.2 7.0 %add_bitcast_fusion = f32[1,224,6144]{2,1,0:T(8,128)} fusion(f32[224,6144]{1,0:T(8,128)} %collective-permute-done, bf16[224,6144]{1,0:T(8,128)(2,1)} %shard_map.85, f32[6144]{0:T(1024)S(1)} %bitcast.58, f32[6144]{0:T(1024)S(1)} %bitcast.57, pred[224]{0:T(512)(128)(4,1)S(1)} %fusion), kind=kLoop, calls=%fused_computation | loop fusion | flops 5505024 | bytes 13811936 | tf_op jit(solution)/shard_map/broadcast_in_dim | solution.py:322
  (48 shorter events, 1.4 us)
Async XLA Ops:
  0.0 15.2 %copy-start = (s32[40,40]{1,0:T(8,128)S(1)}, s32[40,40]{1,0:T(8,128)}, u32[]{:S(2)}) copy-start(s32[40,40]{1,0:T(8,128)} %param.15) | copy-start | bytes 19204
  6.4 32.7 %collective-permute-start.2 = (bf16[224,1536]{1,0:T(8,128)(2,1)}, bf16[224,1536]{1,0:T(8,128)(2,1)}, u32[]{:S(2)}, u32[]{:S(2)}) collective-permute-start(bf16[224,1536]{1,0:T(8,128)(2,1)} %get-tuple-element.37), channel_id=1, source_target_pairs={{0,1},{1,0},{2,3},{3,2},{4,5},{5,4},{6,7},{7,6},{8,9},{9,8},{10,11... | collective-permute-start | bytes 2064392 | tf_op jit(solution)/shard_map/ppermute | solution.py:26
  9.4 49.1 %collective-permute-start.3 = (bf16[224,1536]{1,0:T(8,128)(2,1)}, bf16[224,1536]{1,0:T(8,128)(2,1)}, u32[]{:S(2)}, u32[]{:S(2)}) collective-permute-start(bf16[224,1536]{1,0:T(8,128)(2,1)} %get-tuple-element.36), channel_id=1, source_target_pairs={{0,2},{1,3},{2,0},{3,1},{4,6},{5,7},{6,4},{7,5},{8,10},{9,11},{10,... | collective-permute-start | bytes 2064392 | tf_op jit(solution)/shard_map/ppermute | solution.py:26
  12.0 50.1 %collective-permute-start.4 = (bf16[224,1536]{1,0:T(8,128)(2,1)S(1)}, bf16[224,1536]{1,0:T(8,128)(2,1)}, u32[]{:S(2)}, u32[]{:S(2)}) collective-permute-start(bf16[224,1536]{1,0:T(8,128)(2,1)S(1)} %get-tuple-element.35), channel_id=1, source_target_pairs={{0,3},{1,2},{2,1},{3,0},{4,7},{5,6},{6,5},{7,4},{8,11},{9,10},{10,... | collective-permute-start | bytes 2064392 | tf_op jit(solution)/shard_map/ppermute | solution.py:26
  12.0 4.9 %collective-permute-start.1 = (f32[2,6144]{1,0:T(2,128)}, f32[2,6144]{1,0:T(2,128)S(1)}, u32[]{:S(2)}, u32[]{:S(2)}) collective-permute-start(f32[2,6144]{1,0:T(2,128)} %bitcast.1), channel_id=1, source_target_pairs={{0,4},{4,8},{8,12},{12,16},{16,20},{20,24},{24,28},{28,0},{1,5},{5... | collective-permute-start | bytes 147464 | tf_op jit(solution)/shard_map/ppermute | solution.py:31
  12.0 380.1 %collective-permute-start = (f32[224,6144]{1,0:T(8,128)}, f32[224,6144]{1,0:T(8,128)}, u32[]{:S(2)}, u32[]{:S(2)}) collective-permute-start(f32[224,6144]{1,0:T(8,128)} %bitcast.59), channel_id=1, source_target_pairs={{0,4},{4,8},{8,12},{12,16},{16,20},{20,24},{24,28},{28,0},{1,5},{5... | collective-permute-start | bytes 16515080 | tf_op jit(solution)/shard_map/ppermute | solution.py:31
  39.1 24.2 %slice-start = ((s8[8257536]{0:T(1024)(128)(4,1)}), s8[4194304]{0:T(1024)(128)(4,1)S(1)}, s32[]{:S(2)}) async-start(s8[8257536]{0:T(1024)(128)(4,1)} %bitcast.55), calls=%async_computation | async-start | bytes 8388608
  42.3 21.1 %slice-start.1 = ((s8[8257536]{0:T(1024)(128)(4,1)}), s8[4063232]{0:T(1024)(128)(4,1)S(1)}, s32[]{:S(2)}) async-start(s8[8257536]{0:T(1024)(128)(4,1)} %bitcast.55), calls=%async_computation.1 | async-start | bytes 8126464
  42.7 99.4 %collective-permute-start.8 = (bf16[2,224,768]{2,1,0:T(8,128)(2,1)S(1)}, bf16[2,224,768]{2,1,0:T(8,128)(2,1)S(1)}, u32[]{:S(2)}, u32[]{:S(2)}) collective-permute-start(bf16[2,224,768]{2,1,0:T(8,128)(2,1)S(1)} %pad_maximum_fusion.3), channel_id=1, source_target_pairs={{0,1},{1,0},{2,3},{3,2},{4,5},{5,4},{6,7},{7,6},{8,9},{9,8},{10,11... | collective-permute-start | bytes 2064392 | tf_op jit(solution)/shard_map/ppermute | solution.py:26
  42.8 100.6 %collective-permute-start.9 = (bf16[2,224,768]{2,1,0:T(8,128)(2,1)S(1)}, bf16[2,224,768]{2,1,0:T(8,128)(2,1)S(1)}, u32[]{:S(2)}, u32[]{:S(2)}) collective-permute-start(bf16[2,224,768]{2,1,0:T(8,128)(2,1)S(1)} %pad_maximum_fusion.4), channel_id=1, source_target_pairs={{0,2},{1,3},{2,0},{3,1},{4,6},{5,7},{6,4},{7,5},{8,10},{9,11},{10,... | collective-permute-start | bytes 2064392 | tf_op jit(solution)/shard_map/ppermute | solution.py:26
  58.5 86.5 %collective-permute-start.10 = (bf16[2,224,768]{2,1,0:T(8,128)(2,1)S(1)}, bf16[2,224,768]{2,1,0:T(8,128)(2,1)S(1)}, u32[]{:S(2)}, u32[]{:S(2)}) collective-permute-start(bf16[2,224,768]{2,1,0:T(8,128)(2,1)S(1)} %pad_maximum_fusion.5), channel_id=1, source_target_pairs={{0,3},{1,2},{2,1},{3,0},{4,7},{5,6},{6,5},{7,4},{8,11},{9,10},{10,... | collective-permute-start | bytes 2064392 | tf_op jit(solution)/shard_map/ppermute | solution.py:26
  64.4 89.2 %collective-permute-start.5 = (bf16[2,224,768]{2,1,0:T(8,128)(2,1)S(1)}, bf16[2,224,768]{2,1,0:T(8,128)(2,1)S(1)}, u32[]{:S(2)}, u32[]{:S(2)}) collective-permute-start(bf16[2,224,768]{2,1,0:T(8,128)(2,1)S(1)} %pad_maximum_fusion), channel_id=1, source_target_pairs={{0,1},{1,0},{2,3},{3,2},{4,5},{5,4},{6,7},{7,6},{8,9},{9,8},{10,11... | collective-permute-start | bytes 2064392 | tf_op jit(solution)/shard_map/ppermute | solution.py:26
  139.2 2.5 copy-start.4
  141.6 3.5 copy-start.2
  142.0 34.4 %collective-permute-start.6 = (bf16[2,224,768]{2,1,0:T(8,128)(2,1)S(1)}, bf16[2,224,768]{2,1,0:T(8,128)(2,1)S(1)}, u32[]{:S(2)}, u32[]{:S(2)}) collective-permute-start(bf16[2,224,768]{2,1,0:T(8,128)(2,1)S(1)} %pad_maximum_fusion.1), channel_id=1, source_target_pairs={{0,2},{1,3},{2,0},{3,1},{4,6},{5,7},{6,4},{7,5},{8,10},{9,11},{10,... | collective-permute-start | bytes 2064392 | tf_op jit(solution)/shard_map/ppermute | solution.py:26
  143.4 33.1 %collective-permute-start.7 = (bf16[2,224,768]{2,1,0:T(8,128)(2,1)S(1)}, bf16[2,224,768]{2,1,0:T(8,128)(2,1)S(1)}, u32[]{:S(2)}, u32[]{:S(2)}) collective-permute-start(bf16[2,224,768]{2,1,0:T(8,128)(2,1)S(1)} %pad_maximum_fusion.2), channel_id=1, source_target_pairs={{0,3},{1,2},{2,1},{3,0},{4,7},{5,6},{6,5},{7,4},{8,11},{9,10},{10,... | collective-permute-start | bytes 2064392 | tf_op jit(solution)/shard_map/ppermute | solution.py:26
  176.6 2.6 copy-start.3
  187.5 1.5 copy-start.5
  392.2 7.1 %copy-start.1 = (s32[40,40]{1,0:T(8,128)S(1)}, s32[40,40]{1,0:T(8,128)}, u32[]{:S(2)}) copy-start(s32[40,40]{1,0:T(8,128)} %param.15) | copy-start | bytes 19204

commit v4 on v3

--- a/solution.py
+++ b/solution.py
@@ -15,7 +15,8 @@
 TOKS = 896
 KEYS = 1344
 PAIR = 2 * HDIM
-FLOOR = -3.0e38
+FLOOR = -3.0e37
+TINY = 1.0e-30
 SCALE = HDIM ** (-0.5) * math.log2(math.e)
 COLS = 256
 LAG = 3
@@ -44,36 +45,59 @@
     return lax.dot_general(left, right, (((1,), (1,)), ((), ())), preferred_element_type=jnp.float32)
 
 
-def far_kernel(q_ref, k_ref, v_ref, bias_ref, acc_ref, high_ref, total_ref):
+def lane_of(head):
+    return lax.broadcasted_iota(jnp.int32, (SPAN, HDIM), 1) == head
+
+
+def attend_part(queries, keys, values, bias):
+    scores = dot_t(queries, keys)
+    if bias is not None:
+        scores = scores + bias
+    highest = jnp.maximum(jnp.max(scores, axis=1, keepdims=True), FLOOR) * SCALE
+    raised = jnp.exp2(scores * SCALE - highest)
+    total = jnp.sum(raised, axis=1, keepdims=True)
+    mixed = jnp.dot(raised.astype(jnp.bfloat16), values, preferred_element_type=jnp.float32)
+    return mixed / jnp.maximum(total, TINY), highest + jnp.log2(total)
+
+
+def far_kernel(q_ref, k_ref, v_ref, bias_ref, out_ref, level_ref):
+    step = pl.program_id(1)
+
+    @pl.when(step == 0)
+    def _():
+        level_ref[...] = jnp.zeros_like(level_ref)
+
     for head in range(2):
         cols = slice(head * HDIM, (head + 1) * HDIM)
-        scores = dot_t(q_ref[:, cols], k_ref[0, 0, 0, :, cols]) + bias_ref[0:1, :]
-        highest = jnp.maximum(jnp.max(scores, axis=1, keepdims=True), FLOOR)
-        raised = jnp.exp2(scores * SCALE - highest * SCALE)
-        total = jnp.sum(raised, axis=1, keepdims=True)
-        acc_ref[:, cols] = jnp.dot(
-            raised.astype(jnp.bfloat16), v_ref[0, 0, 0, :, cols], preferred_element_type=jnp.float32
+        mixed, level = attend_part(
+            q_ref[:, cols], k_ref[0, 0, 0, :, cols], v_ref[0, 0, 0, :, cols], bias_ref[0:1, :]
         )
-        high_ref[:, cols] = jnp.broadcast_to(highest, (SPAN, HDIM))
-        total_ref[:, cols] = jnp.broadcast_to(total, (SPAN, HDIM))
-
-
-def near_kernel(q_ref, k_ref, v_ref, acc_ref, high_ref, total_ref, *rest):
-    out_ref = rest[-1]
+        out_ref[:, cols] = mixed
+        level_ref[...] = jnp.where(lane_of(2 * step + head), level, level_ref[...])
+
+
+def near_kernel(q_ref, k_ref, v_ref, out_ref, level_ref):
+    step = pl.program_id(0)
+
+    @pl.when(step == 0)
+    def _():
+        level_ref[...] = jnp.zeros_like(level_ref)
+
     for head in range(2):
         cols = slice(head * HDIM, (head + 1) * HDIM)
-        scores = dot_t(q_ref[:, cols], k_ref[0, :, cols])
-        far_high = high_ref[:, cols]
-        near_high = jnp.broadcast_to(jnp.max(scores, axis=1, keepdims=True), (SPAN, HDIM))
-        highest = jnp.maximum(near_high, far_high) * SCALE
-        wide = jnp.concatenate([highest] * -(-SPAN // HDIM), axis=1)[:, :SPAN]
-        raised = jnp.exp2(scores * SCALE - wide)
-        fade = jnp.exp2(far_high * SCALE - highest)
-        near_total = jnp.broadcast_to(jnp.sum(raised, axis=1, keepdims=True), (SPAN, HDIM))
-        total = near_total + total_ref[:, cols] * fade
-        mixed = jnp.dot(raised.astype(jnp.bfloat16), v_ref[0, :, cols], preferred_element_type=jnp.float32)
-        mixed = (mixed + acc_ref[:, cols] * fade) / total
+        mixed, level = attend_part(q_ref[:, cols], k_ref[0, :, cols], v_ref[0, :, cols], None)
         out_ref[:, cols] = mixed.astype(jnp.bfloat16)
+        level_ref[...] = jnp.where(lane_of(2 * step + head), level, level_ref[...])
+
+
+def join_kernel(far_ref, far_level_ref, near_ref, near_level_ref, out_ref):
+    step = pl.program_id(1)
+    share = 1.0 / (1.0 + jnp.exp2(far_level_ref[...] - near_level_ref[...]))
+    for head in range(2):
+        cols = slice(head * HDIM, (head + 1) * HDIM)
+        part = jnp.sum(jnp.where(lane_of(2 * step + head), share, 0.0), axis=1, keepdims=True)
+        far = far_ref[:, cols]
+        out_ref[:, cols] = (far + (near_ref[:, cols].astype(jnp.float32) - far) * part).astype(jnp.bfloat16)
 
 
 def far_mix(queries, cache_kv, live_slots):
@@ -90,48 +114,56 @@
             pl.BlockSpec((1, 1, 1, KEYS, PAIR), lambda b, h: (0, 1, b, 0, h)),
             pl.BlockSpec((8, KEYS), lambda b, h: (0, 0)),
         ],
-        out_specs=[block] * 3,
-        out_shape=[jax.ShapeDtypeStruct((TOKS, width), jnp.float32)] * 3,
+        out_specs=[block, pl.BlockSpec((SPAN, HDIM), lambda b, h: (b, 0))],
+        out_shape=[
+            jax.ShapeDtypeStruct((TOKS, width), jnp.float32),
+            jax.ShapeDtypeStruct((TOKS, HDIM), jnp.float32),
+        ],
         compiler_params=pltpu.CompilerParams(vmem_limit_bytes=40 * 1024 * 1024),
         cost_estimate=pl.CostEstimate(
-            flops=4 * TOKS * KEYS * width,
-            bytes_accessed=TOKS * width,
-            transcendentals=0,
+            flops=4 * TOKS * KEYS * width, bytes_accessed=TOKS * width, transcendentals=0
         ),
     )(queries, cache_kv, cache_kv, bias)
 
 
-def near_mix(queries, own_kv, far_parts, first, earlier):
-    width, group = queries.shape[1], own_kv.shape[2]
-    block = pl.BlockSpec((SPAN, PAIR), lambda b, h: (b, h + first))
-    operands = [queries, own_kv, own_kv, *far_parts]
-    in_specs = [
-        block,
-        pl.BlockSpec((1, SPAN, PAIR), lambda b, h: (0, b, h)),
-        pl.BlockSpec((1, SPAN, PAIR), lambda b, h: (1, b, h)),
-        block,
-        block,
-        block,
-    ]
-    aliases = {}
-    if earlier is not None:
-        aliases = {len(operands): 0}
-        operands.append(earlier)
-        in_specs.append(pl.BlockSpec(memory_space=pl.ANY))
+def near_mix(queries, own_kv):
+    width = queries.shape[1]
+    block = pl.BlockSpec((SPAN, PAIR), lambda h: (0, h))
     return pl.pallas_call(
         near_kernel,
-        grid=(VIDS, group // PAIR),
-        in_specs=in_specs,
+        grid=(width // PAIR,),
+        in_specs=[
+            block,
+            pl.BlockSpec((1, SPAN, PAIR), lambda h: (0, 0, h)),
+            pl.BlockSpec((1, SPAN, PAIR), lambda h: (1, 0, h)),
+        ],
+        out_specs=[block, pl.BlockSpec((SPAN, HDIM), lambda h: (0, 0))],
+        out_shape=[
+            jax.ShapeDtypeStruct((SPAN, width), jnp.bfloat16),
+            jax.ShapeDtypeStruct((SPAN, HDIM), jnp.float32),
+        ],
+        compiler_params=pltpu.CompilerParams(vmem_limit_bytes=40 * 1024 * 1024),
+        cost_estimate=pl.CostEstimate(
+            flops=4 * SPAN * SPAN * width, bytes_accessed=SPAN * width, transcendentals=0
+        ),
+    )(queries, own_kv, own_kv)
+
+
+def join(far, far_level, near, near_level):
+    width = far.shape[1]
+    block = pl.BlockSpec((SPAN, PAIR), lambda b, h: (b, h))
+    level = pl.BlockSpec((SPAN, HDIM), lambda b, h: (b, 0))
+    return pl.pallas_call(
+        join_kernel,
+        grid=(VIDS, width // PAIR),
+        in_specs=[block, level, block, level],
         out_specs=block,
         out_shape=jax.ShapeDtypeStruct((TOKS, width), jnp.bfloat16),
-        input_output_aliases=aliases,
         compiler_params=pltpu.CompilerParams(vmem_limit_bytes=40 * 1024 * 1024),
         cost_estimate=pl.CostEstimate(
-            flops=4 * TOKS * SPAN * group,
-            bytes_accessed=TOKS * group,
-            transcendentals=0,
-        ),
-    )(*operands)
+            flops=TOKS * width, bytes_accessed=TOKS * width, transcendentals=0
+        ),
+    )(far, far_level, near, near_level)
 
 
 def flipped(place, bits):
@@ -271,48 +303,64 @@
     )(heads_all, out_proj)
 
 
-def heads_gathered(cut, rows, place, devices):
+def rows_gathered(cut, rows, place, group):
     piece = cut(place)
-    whole = jnp.zeros(piece.shape[:-2] + (rows * devices, piece.shape[-1]), piece.dtype)
+    whole = jnp.zeros(piece.shape[:-2] + (rows * group, piece.shape[-1]), piece.dtype)
     lead = (0,) * (piece.ndim - 2)
-    near_piece = piece
-    for bit in range(devices):
+    for bit in range(group):
         other = place ^ bit
         piece = cut(other)
         if bit:
             piece = swapped(piece, "sp", bit)
-        if bit == 1:
-            near_piece = piece
-        whole = lax.dynamic_update_slice(whole, piece, (*lead, other * rows, 0))
-    return whole, near_piece
+        whole = lax.dynamic_update_slice(whole, piece, (*lead, other % group * rows, 0))
+    return whole
+
+
+def both_videos(own, other, video):
+    whole = jnp.zeros((TOKS, own.shape[1]), own.dtype)
+    whole = lax.dynamic_update_slice(whole, own, (video * SPAN, 0))
+    return lax.dynamic_update_slice(whole, other, ((1 - video) * SPAN, 0))
 
 
 def per_device(resid, qkv, cache_kv, out_proj, gate, span_ids, cache_counts, span_mask):
     own_rows = resid.shape[1]
     width = cache_kv.shape[4]
+    heads = width // HDIM
     devices = lax.axis_size("sp")
+    group = devices // VIDS
     place = lax.axis_index("sp")
+    video = place // group
     live_slots = visible_slots(span_ids[0], cache_counts[0], span_mask)
 
-    def cut_queries(other):
-        return lax.dynamic_slice(qkv[0, :, 0], (0, other * width), (own_rows, width))
-
-    queries, near_piece = heads_gathered(cut_queries, own_rows, place, devices)
-    far_parts = far_mix(queries, cache_kv, live_slots)
-
-    pairs = width // PAIR
-    front = (pairs + 1) // 2
-    heads_all = None
-    for first, count, awaited in ((0, front, near_piece), (front, pairs - front, queries)):
-        source, _ = lax.optimization_barrier((qkv, awaited))
-
-        def cut_kv(other):
-            begin = (0, other * width + first * PAIR)
-            size = (own_rows, count * PAIR)
-            return jnp.stack([lax.dynamic_slice(source[0, :, i], begin, size) for i in (1, 2)])
-
-        own_kv, _ = heads_gathered(cut_kv, own_rows, place, devices)
-        heads_all = near_mix(queries, own_kv, far_parts, first, heads_all)
+    def gathered(across, parts, source):
+        def cut(other):
+            holder = other ^ group if across else other
+            begin, size = (0, holder * width), (own_rows, width)
+            cuts = [lax.dynamic_slice(source[0, :, i], begin, size) for i in parts]
+            return cuts[0] if len(cuts) == 1 else jnp.stack(cuts)
+
+        return rows_gathered(cut, own_rows, place, group)
+
+    across_q = gathered(True, (0,), qkv)
+    other_q = swapped(across_q, "sp", group)
+    source, _ = lax.optimization_barrier((qkv, across_q))
+    across_kv = gathered(True, (1, 2), source)
+    source, _ = lax.optimization_barrier((qkv, across_kv))
+    own_q = gathered(False, (0,), source)
+    own_kv = gathered(False, (1, 2), source)
+
+    across_out, across_level = near_mix(across_q, across_kv)
+    other_out = swapped(across_out, "sp", group)
+    other_level = swapped(across_level[:, :heads].T, "sp", group).T
+    other_level = jnp.pad(other_level, ((0, 0), (0, HDIM - heads)))
+
+    queries = both_videos(own_q, other_q, video)
+    queries, _ = lax.optimization_barrier((queries, across_out))
+    far, far_level = far_mix(queries, cache_kv, live_slots)
+    own_out, own_level = near_mix(own_q, own_kv)
+    near = both_videos(own_out, other_out, video)
+    near_level = both_videos(own_level, other_level, video)
+    heads_all = join(far, far_level, near, near_level)
 
     resid_prev = passed_along(resid[0], "section", 1)
     gate_prev = passed_along(gate[0], "section", 1)

time: 400 us -> 402 us (level)
  waiting for transfers between devices: 55.7 us -> 126 us
  starting transfers between devices: 57.6 us -> 12.8 us
  local copies, waits for them, and re-layouts: 23 us -> 10.9 us
  Pallas kernels: 253 us -> 242 us
    ppermute x9 -> x7, waiting for transfers between devices: 55.7 us -> 126 us  [swapped(): return lax.ppermute(shard, axis, [(i, i ^ bit) for i in range(devices)])]
    ppermute x9 -> x7, starting transfers between devices: 55.8 us -> 11.2 us  [swapped(): return lax.ppermute(shard, axis, [(i, i ^ bit) for i in range(devices)])]
    pallas_call x1, Pallas kernels: 203 us -> 191 us  [summed_and_moved(): pl.pallas_call(lambda *refs: sum_kernel(devices, *refs), out_shape=jax.Sh...]
    unnamed x16 -> x10, local copies, waits for them, and re-layouts: 6.58 us -> 1.56 us
    pallas_call x2 -> x3, Pallas kernels: 16.8 us -> 17 us  [the longest x2 13.5 us: near_mix(): pl.pallas_call(near_kernel, grid=(width // PAIR,), in_specs=[block, pl.Bl...]
  transfers between devices with their start and end apart: 11 -> 9, of which waited for: 3 -> 4; matrix products, arithmetic and copies ran while one was open for 3% -> 2% of each run, Pallas kernels for 63% -> 60%
where the time goes in v4:
time: 402 us; the launch traced here: 401 us
  Pallas kernels  242 us (60%)
  waiting for transfers between devices  126 us (31%)
  starting transfers between devices  12.8 us (3%)
  local copies, waits for them, and re-layouts  10.9 us (3%)
  other arithmetic  7.83 us (2%)
    pallas_call x1, Pallas kernels, summed_and_moved(): pl.pallas_call(lambda *refs: sum_kernel(devices, *refs), out_shape=jax.Sh...  191 us
    ppermute x7, waiting for transfers between devices, swapped(): return lax.ppermute(shard, axis, [(i, i ^ bit) for i in range(devices)])  126 us
    pallas_call x1, Pallas kernels, far_mix(): pl.pallas_call(far_kernel, grid=(VIDS, width // PAIR), in_specs=[block, p...  33.2 us
    pallas_call x2, Pallas kernels, near_mix(): pl.pallas_call(near_kernel, grid=(width // PAIR,), in_specs=[block, pl.Bl...  13.5 us
    ppermute x7, starting transfers between devices, swapped(): return lax.ppermute(shard, axis, [(i, i ^ bit) for i in range(devices)])  11.2 us
  transfers between devices with their start and end apart: 9, of which 4 were waited for; matrix products, arithmetic and copies ran while one was open for 2% of the time, Pallas kernels for 60%

profile of v4, /device:TPU:0, one launch (start us, length us, event | category | flops | bytes accessed | tf_op | source)
XLA Modules:
  0.0 401.2 jit_solution(1434073294819018365)
XLA Ops:
  0.0 2.1 slice.35
  2.1 0.9 dynamic-slice_bitcast_fusion.9
  3.0 3.0 collective-permute-start.2
  6.0 1.6 collective-permute-start
  9.0 0.2 select_reduce_fusion
  9.5 12.2 %collective-permute-done.2 = bf16[224,1536]{1,0:T(8,128)(2,1)S(1)} collective-permute-done((bf16[224,1536]{1,0:T(8,128)(2,1)}, bf16[224,1536]{1,0:T(8,128)(2,1)S(1)}, u32[]{:S(2)}, u32[]{:S(2)}) %collective-permute-start.2) | collective-permute-done | bytes 688160 | tf_op jit(solution)/shard_map/ppermute | solution.py:27
  21.7 3.0 fusion.3
  24.7 0.2 dynamic-slice_bitcast_fusion.5
  25.1 1.8 collective-permute-start.3
  26.9 2.7 collective-permute-start.5
  29.6 0.2 broadcast.70.clone
  29.8 0.2 maximum_dynamic-update-slice_fusion
  29.9 55.9 %collective-permute-done.3 = bf16[2,224,1536]{2,1,0:T(8,128)(2,1)S(1)} collective-permute-done((bf16[2,224,1536]{2,1,0:T(8,128)(2,1)S(1)}, bf16[2,224,1536]{2,1,0:T(8,128)(2,1)S(1)}, u32[]{:S(2)}, u32[]{:S(2)}) %collective-permute-start.3) | collective-permute-done | bytes 1376288 | tf_op jit(solution)/shard_map/ppermute | solution.py:27
  86.0 0.7 fusion.2
  87.2 2.1 collective-permute-start.4
  89.3 6.8 %shard_map.82 = (bf16[448,1536]{1,0:T(8,128)(2,1)S(1)}, f32[448,128]{1,0:T(8,128)S(1)}) custom-call(bf16[448,1536]{1,0:T(8,128)(2,1)S(1)} %constant_dynamic-update-slice_fusion.7.q_ref, bf16[2,448,1536]{2,1,0:T(8,128)(2,1)S(1)} %constant_dynamic-update-slice_fusion.6.k_ref.v_ref, bf16[2,448,1536]{2,1,0:T(8,128)(2,1)S(1)} %constant_dynamic-update-slice_fusion.6.k_ref.v_ref), custom_call_target="tpu_custom_call" | custom-call | flops 1233125376 | bytes 688128 | tf_op jit(solution)/shard_map/pallas_call | solution.py:132
  96.1 1.0 collective-permute-start.8
  97.2 0.2 broadcast.70
  97.4 0.1 maximum_dynamic-update-slice_fusion.1
  97.6 39.9 %collective-permute-done.4 = bf16[224,1536]{1,0:T(8,128)(2,1)S(1)} collective-permute-done((bf16[224,1536]{1,0:T(8,128)(2,1)S(1)}, bf16[224,1536]{1,0:T(8,128)(2,1)S(1)}, u32[]{:S(2)}, u32[]{:S(2)}) %collective-permute-start.4) | collective-permute-done | bytes 688160 | tf_op jit(solution)/shard_map/ppermute | solution.py:27
  137.5 0.6 collective-permute-start.7
  138.1 0.2 broadcast.68.clone
  138.3 0.1 constant_dynamic-update-slice_fusion.4
  138.6 33.2 %shard_map.83 = (f32[896,1536]{1,0:T(8,128)S(1)}, f32[896,128]{1,0:T(8,128)S(1)}) custom-call(bf16[896,1536]{1,0:T(8,128)(2,1)S(1)} %constant_dynamic-update-slice_fusion.3.q_ref, bf16[1,2,2,1344,1536]{4,3,2,1,0:T(8,128)(2,1)} %v_ref.1, bf16[1,2,2,1344,1536]{4,3,2,1,0:T(8,128)(2,1)} %v_ref.1, f32[8,1344]{1,0:T(8,128)S(1)} %broadcast_in_dim.80.bias_ref), custom_call_target="tpu_custom_call" | custom-call | flops 7398752256 | bytes 1376256 | tf_op jit(solution)/shard_map/pallas_call | solution.py:108
  171.8 0.1 constant_dynamic-update-slice_fusion.2.k_ref.v_ref
  172.0 6.8 %shard_map.84 = (bf16[448,1536]{1,0:T(8,128)(2,1)S(1)}, f32[448,128]{1,0:T(8,128)S(1)}) custom-call(bf16[448,1536]{1,0:T(8,128)(2,1)S(1)} %constant_dynamic-update-slice_fusion.5.q_ref, bf16[2,448,1536]{2,1,0:T(8,128)(2,1)S(1)} %constant_dynamic-update-slice_fusion.2.k_ref.v_ref, bf16[2,448,1536]{2,1,0:T(8,128)(2,1)S(1)} %constant_dynamic-update-slice_fusion.2.k_ref.v_ref), custom_call_target="tpu_custom_call" | custom-call | flops 1233125376 | bytes 688128 | tf_op jit(solution)/shard_map/pallas_call | solution.py:132
  178.9 0.2 broadcast.68.clone.1
  179.2 18.3 %collective-permute-done.7 = bf16[448,1536]{1,0:T(8,128)(2,1)S(1)} collective-permute-done((bf16[448,1536]{1,0:T(8,128)(2,1)S(1)}, bf16[448,1536]{1,0:T(8,128)(2,1)S(1)}, u32[]{:S(2)}, u32[]{:S(2)}) %collective-permute-start.7) | collective-permute-done | bytes 1376288 | tf_op jit(solution)/shard_map/ppermute | solution.py:27
  197.7 3.5 shard_map.85.refs_0_
  201.2 1.5 copy-done.2
  202.7 191.4 %shard_map.86 = bf16[224,6144]{1,0:T(8,128)(2,1)} custom-call(bf16[896,1536]{1,0:T(8,128)(2,1)} %copy-done.2, bf16[1,1536,6144]{2,1,0:T(8,128)(2,1)} %refs_1_.1), custom_call_target="tpu_custom_call" | custom-call | flops 16911433728 | bytes 18874368 | tf_op jit(solution)/shard_map/pallas_call | solution.py:281
  394.2 7.1 %add_bitcast_fusion = f32[1,224,6144]{2,1,0:T(8,128)} fusion(f32[224,6144]{1,0:T(8,128)} %collective-permute-done, bf16[224,6144]{1,0:T(8,128)(2,1)} %shard_map.86, f32[6144]{0:T(1024)S(1)} %bitcast.46, f32[6144]{0:T(1024)S(1)} %bitcast.45, pred[224]{0:T(512)(128)(4,1)S(1)} %fusion), kind=kLoop, calls=%fused_computation | loop fusion | flops 5505024 | bytes 13811936 | tf_op jit(solution)/shard_map/broadcast_in_dim | solution.py:370
  (44 shorter events, 1.9 us)
Async XLA Ops:
  0.0 8.9 %copy-start = (s32[40,40]{1,0:T(8,128)S(1)}, s32[40,40]{1,0:T(8,128)}, u32[]{:S(2)}) copy-start(s32[40,40]{1,0:T(8,128)} %param.15) | copy-start | bytes 19204
  3.0 18.7 %collective-permute-start.2 = (bf16[224,1536]{1,0:T(8,128)(2,1)}, bf16[224,1536]{1,0:T(8,128)(2,1)S(1)}, u32[]{:S(2)}, u32[]{:S(2)}) collective-permute-start(bf16[224,1536]{1,0:T(8,128)(2,1)} %dynamic-slice_bitcast_fusion.9), channel_id=1, source_target_pairs={{0,1},{1,0},{2,3},{3,2},{4,5},{5,4},{6,7},{7,6},{8,9},{9,8},{10,11... | collective-permute-start | bytes 2064392 | tf_op jit(solution)/shard_map/ppermute | solution.py:27
  6.0 20.9 %collective-permute-start.1 = (f32[2,6144]{1,0:T(2,128)}, f32[2,6144]{1,0:T(2,128)S(1)}, u32[]{:S(2)}, u32[]{:S(2)}) collective-permute-start(f32[2,6144]{1,0:T(2,128)} %bitcast.48), channel_id=1, source_target_pairs={{0,4},{4,8},{8,12},{12,16},{16,20},{20,24},{24,28},{28,0},{1,5},{5... | collective-permute-start | bytes 147464 | tf_op jit(solution)/shard_map/ppermute | solution.py:32
  6.0 388.1 %collective-permute-start = (f32[224,6144]{1,0:T(8,128)}, f32[224,6144]{1,0:T(8,128)}, u32[]{:S(2)}, u32[]{:S(2)}) collective-permute-start(f32[224,6144]{1,0:T(8,128)} %bitcast.47), channel_id=1, source_target_pairs={{0,4},{4,8},{8,12},{12,16},{16,20},{20,24},{24,28},{28,0},{1,5},{5... | collective-permute-start | bytes 16515080 | tf_op jit(solution)/shard_map/ppermute | solution.py:32
  24.7 61.3 %slice-start = ((s8[8257536]{0:T(1024)(128)(4,1)}), s8[4194304]{0:T(1024)(128)(4,1)S(1)}, s32[]{:S(2)}) async-start(s8[8257536]{0:T(1024)(128)(4,1)} %bitcast.42), calls=%async_computation | async-start | bytes 8388608
  25.1 61.0 %slice-start.1 = ((s8[8257536]{0:T(1024)(128)(4,1)}), s8[4063232]{0:T(1024)(128)(4,1)S(1)}, s32[]{:S(2)}) async-start(s8[8257536]{0:T(1024)(128)(4,1)} %bitcast.42), calls=%async_computation.1 | async-start | bytes 8126464
  25.1 60.8 %collective-permute-start.3 = (bf16[2,224,1536]{2,1,0:T(8,128)(2,1)S(1)}, bf16[2,224,1536]{2,1,0:T(8,128)(2,1)S(1)}, u32[]{:S(2)}, u32[]{:S(2)}) collective-permute-start(bf16[2,224,1536]{2,1,0:T(8,128)(2,1)S(1)} %pad_maximum_fusion), channel_id=1, source_target_pairs={{0,1},{1,0},{2,3},{3,2},{4,5},{5,4},{6,7},{7,6},{8,9},{9,8},{10,11... | collective-permute-start | bytes 4128776 | tf_op jit(solution)/shard_map/ppermute | solution.py:27
  26.9 111.6 %collective-permute-start.5 = (bf16[448,1536]{1,0:T(8,128)(2,1)S(1)}, bf16[448,1536]{1,0:T(8,128)(2,1)S(1)}, u32[]{:S(2)}, u32[]{:S(2)}) collective-permute-start(bf16[448,1536]{1,0:T(8,128)(2,1)S(1)} %constant_dynamic-update-slice_fusion.7.q_ref), channel_id=1, source_target_pairs={{0,2},{1,3},{2,0},{3,1},{4,6},{5,7},{6,4},{7,5},{8,10},{9,11},{10,... | collective-permute-start | bytes 4128776 | tf_op jit(solution)/shard_map/ppermute | solution.py:27
  87.1 84.7 %collective-permute-start.6 = (bf16[2,224,1536]{2,1,0:T(8,128)(2,1)S(1)}, bf16[2,224,1536]{2,1,0:T(8,128)(2,1)S(1)}, u32[]{:S(2)}, u32[]{:S(2)}) collective-permute-start(bf16[2,224,1536]{2,1,0:T(8,128)(2,1)S(1)} %pad_maximum_fusion.1), channel_id=1, source_target_pairs={{0,1},{1,0},{2,3},{3,2},{4,5},{5,4},{6,7},{7,6},{8,9},{9,8},{10,11... | collective-permute-start | bytes 4128776 | tf_op jit(solution)/shard_map/ppermute | solution.py:27
  87.2 50.2 %collective-permute-start.4 = (bf16[224,1536]{1,0:T(8,128)(2,1)S(1)}, bf16[224,1536]{1,0:T(8,128)(2,1)S(1)}, u32[]{:S(2)}, u32[]{:S(2)}) collective-permute-start(bf16[224,1536]{1,0:T(8,128)(2,1)S(1)} %dynamic-slice_bitcast_fusion.4), channel_id=1, source_target_pairs={{0,1},{1,0},{2,3},{3,2},{4,5},{5,4},{6,7},{7,6},{8,9},{9,8},{10,11... | collective-permute-start | bytes 2064392 | tf_op jit(solution)/shard_map/ppermute | solution.py:27
  96.1 82.7 %collective-permute-start.8 = (f32[12,448]{0,1:T(8,128)S(1)}, f32[12,448]{0,1:T(8,128)S(1)}, u32[]{:S(2)}, u32[]{:S(2)}) collective-permute-start(f32[12,448]{0,1:T(8,128)S(1)} %slice_bitcast_fusion), channel_id=1, source_target_pairs={{0,2},{1,3},{2,0},{3,1},{4,6},{5,7},{6,4},{7,5},{8,10},{9,11},{10,... | collective-permute-start | bytes 64520 | tf_op jit(solution)/shard_map/ppermute | solution.py:27
  137.5 60.1 %collective-permute-start.7 = (bf16[448,1536]{1,0:T(8,128)(2,1)S(1)}, bf16[448,1536]{1,0:T(8,128)(2,1)S(1)}, u32[]{:S(2)}, u32[]{:S(2)}) collective-permute-start(bf16[448,1536]{1,0:T(8,128)(2,1)S(1)} %get-tuple-element.16), channel_id=1, source_target_pairs={{0,2},{1,3},{2,0},{3,1},{4,6},{5,7},{6,4},{7,5},{8,10},{9,11},{10,... | collective-permute-start | bytes 4128776 | tf_op jit(solution)/shard_map/ppermute | solution.py:27
  201.2 1.5 copy-start.2
  394.2 7.1 %copy-start.1 = (s32[40,40]{1,0:T(8,128)S(1)}, s32[40,40]{1,0:T(8,128)}, u32[]{:S(2)}) copy-start(s32[40,40]{1,0:T(8,128)} %param.15) | copy-start | bytes 19204

commit v5 on v4

--- a/solution.py
+++ b/solution.py
@@ -362,8 +362,9 @@
     near_level = both_videos(own_level, other_level, video)
     heads_all = join(far, far_level, near, near_level)
 
-    resid_prev = passed_along(resid[0], "section", 1)
-    gate_prev = passed_along(gate[0], "section", 1)
+    resid_late, gate_late, _ = lax.optimization_barrier((resid, gate, heads_all))
+    resid_prev = passed_along(resid_late[0], "section", 1)
+    gate_prev = passed_along(gate_late[0], "section", 1)
     moved = summed_and_moved(heads_all, out_proj, devices).astype(jnp.float32)
     video_of = (place * own_rows + jnp.arange(own_rows, dtype=jnp.int32)) // SPAN
     gains = jnp.where((video_of == 0)[:, None], gate_prev[0:1], gate_prev[1:2])

time: 402 us -> 418 us (1.040)
  waiting for transfers between devices: 126 us -> 135 us
  local copies, waits for them, and re-layouts: 10.9 us -> 16.5 us
    ppermute x7, waiting for transfers between devices: 126 us -> 135 us  [swapped(): return lax.ppermute(shard, axis, [(i, i ^ bit) for i in range(devices)])]
  transfers between devices with their start and end apart: 9 -> 9, of which waited for: 4 -> 3; matrix products, arithmetic and copies ran while one was open for 2% -> 2% of each run, Pallas kernels for 60% -> 57%
where the time goes in v5:
time: 418 us; the launch traced here: 417 us
  Pallas kernels  242 us (58%)
  waiting for transfers between devices  135 us (32%)
  local copies, waits for them, and re-layouts  16.5 us (4%)
  starting transfers between devices  13.7 us (3%)
  other arithmetic  8.88 us (2%)
    pallas_call x1, Pallas kernels, summed_and_moved(): pl.pallas_call(lambda *refs: sum_kernel(devices, *refs), out_shape=jax.Sh...  192 us
    ppermute x7, waiting for transfers between devices, swapped(): return lax.ppermute(shard, axis, [(i, i ^ bit) for i in range(devices)])  135 us
    pallas_call x1, Pallas kernels, far_mix(): pl.pallas_call(far_kernel, grid=(VIDS, width // PAIR), in_specs=[block, p...  33.2 us
    pallas_call x2, Pallas kernels, near_mix(): pl.pallas_call(near_kernel, grid=(width // PAIR,), in_specs=[block, pl.Bl...  13.5 us
    ppermute x7, starting transfers between devices, swapped(): return lax.ppermute(shard, axis, [(i, i ^ bit) for i in range(devices)])  12.5 us
    slice x3, local copies, waits for them, and re-layouts, cut(): cuts = [lax.dynamic_slice(source[0, :, i], begin, size) for i in parts]  8.72 us
  transfers between devices with their start and end apart: 9, of which 3 were waited for; matrix products, arithmetic and copies ran while one was open for 2% of the time, Pallas kernels for 57%

profile of v5, /device:TPU:0, one launch (start us, length us, event | category | flops | bytes accessed | tf_op | source)
XLA Modules:
  0.0 417.3 jit_solution(17297727365181938909)
XLA Ops:
  0.0 2.0 slice.33
  2.0 1.0 dynamic-slice_bitcast_fusion.9
  3.0 3.0 collective-permute-start
  6.1 1.2 bitcast_dynamic-update-slice_fusion.1
  7.3 14.4 %collective-permute-done = bf16[224,1536]{1,0:T(8,128)(2,1)S(1)} collective-permute-done((bf16[224,1536]{1,0:T(8,128)(2,1)}, bf16[224,1536]{1,0:T(8,128)(2,1)S(1)}, u32[]{:S(2)}, u32[]{:S(2)}) %collective-permute-start) | collective-permute-done | bytes 688160 | tf_op jit(solution)/shard_map/ppermute | solution.py:27
  21.7 3.0 fusion.3
  24.7 0.2 dynamic-slice_bitcast_fusion.5
  24.9 1.2 pad_maximum_fusion
  26.1 1.7 collective-permute-start.1
  29.2 0.2 select_reduce_fusion
  29.6 2.6 collective-permute-start.3
  32.2 0.2 broadcast.69.clone
  32.3 0.1 maximum_dynamic-update-slice_fusion
  32.5 53.2 %collective-permute-done.1 = bf16[2,224,1536]{2,1,0:T(8,128)(2,1)} collective-permute-done((bf16[2,224,1536]{2,1,0:T(8,128)(2,1)}, bf16[2,224,1536]{2,1,0:T(8,128)(2,1)}, u32[]{:S(2)}, u32[]{:S(2)}) %collective-permute-start.1) | collective-permute-done | bytes 1376288 | tf_op jit(solution)/shard_map/ppermute | solution.py:27
  85.7 1.5 constant_dynamic-update-slice_fusion.7.k_ref.v_ref
  87.2 3.8 fusion.2
  91.5 2.1 collective-permute-start.2
  93.5 6.8 %shard_map.82 = (bf16[448,1536]{1,0:T(8,128)(2,1)S(1)}, f32[448,128]{1,0:T(8,128)S(1)}) custom-call(bf16[448,1536]{1,0:T(8,128)(2,1)S(1)} %constant_dynamic-update-slice_fusion.8.q_ref, bf16[2,448,1536]{2,1,0:T(8,128)(2,1)S(1)} %constant_dynamic-update-slice_fusion.7.k_ref.v_ref, bf16[2,448,1536]{2,1,0:T(8,128)(2,1)S(1)} %constant_dynamic-update-slice_fusion.7.k_ref.v_ref), custom_call_target="tpu_custom_call" | custom-call | flops 1233125376 | bytes 688128 | tf_op jit(solution)/shard_map/pallas_call | solution.py:132
  100.3 1.0 collective-permute-start.6
  101.3 2.0 collective-permute-start.5
  103.5 0.2 broadcast.69
  103.7 0.1 maximum_dynamic-update-slice_fusion.1
  103.8 67.2 %collective-permute-done.2 = bf16[224,1536]{1,0:T(8,128)(2,1)S(1)} collective-permute-done((bf16[224,1536]{1,0:T(8,128)(2,1)S(1)}, bf16[224,1536]{1,0:T(8,128)(2,1)S(1)}, u32[]{:S(2)}, u32[]{:S(2)}) %collective-permute-start.2) | collective-permute-done | bytes 688160 | tf_op jit(solution)/shard_map/ppermute | solution.py:27
  171.0 0.2 broadcast.67.clone
  171.5 33.2 %shard_map.83 = (f32[896,1536]{1,0:T(8,128)S(1)}, f32[896,128]{1,0:T(8,128)S(1)}) custom-call(bf16[896,1536]{1,0:T(8,128)(2,1)S(1)} %constant_dynamic-update-slice_fusion.4.q_ref, bf16[1,2,2,1344,1536]{4,3,2,1,0:T(8,128)(2,1)} %v_ref.1, bf16[1,2,2,1344,1536]{4,3,2,1,0:T(8,128)(2,1)} %v_ref.1, f32[8,1344]{1,0:T(8,128)S(1)} %broadcast_in_dim.75.bias_ref), custom_call_target="tpu_custom_call" | custom-call | flops 7398752256 | bytes 1376256 | tf_op jit(solution)/shard_map/pallas_call | solution.py:108
  204.9 6.8 %shard_map.84 = (bf16[448,1536]{1,0:T(8,128)(2,1)S(1)}, f32[448,128]{1,0:T(8,128)S(1)}) custom-call(bf16[448,1536]{1,0:T(8,128)(2,1)S(1)} %constant_dynamic-update-slice_fusion.6.q_ref, bf16[2,448,1536]{2,1,0:T(8,128)(2,1)S(1)} %constant_dynamic-update-slice_fusion.3.k_ref.v_ref, bf16[2,448,1536]{2,1,0:T(8,128)(2,1)S(1)} %constant_dynamic-update-slice_fusion.3.k_ref.v_ref), custom_call_target="tpu_custom_call" | custom-call | flops 1233125376 | bytes 688128 | tf_op jit(solution)/shard_map/pallas_call | solution.py:132
  211.8 0.2 broadcast.67.clone.1
  212.3 3.5 shard_map.85.refs_0_
  215.8 1.5 copy-done.2
  217.3 1.2 collective-permute-start.8
  218.5 191.6 %shard_map.86 = bf16[224,6144]{1,0:T(8,128)(2,1)} custom-call(bf16[896,1536]{1,0:T(8,128)(2,1)} %copy-done.2, bf16[1,1536,6144]{2,1,0:T(8,128)(2,1)} %refs_1_.1), custom_call_target="tpu_custom_call" | custom-call | flops 16911433728 | bytes 18874368 | tf_op jit(solution)/shard_map/pallas_call | solution.py:281
  410.2 7.1 %add_bitcast_fusion = f32[1,224,6144]{2,1,0:T(8,128)} fusion(f32[224,6144]{1,0:T(8,128)} %collective-permute-done.7, bf16[224,6144]{1,0:T(8,128)(2,1)} %shard_map.86, f32[6144]{0:T(1024)S(1)} %bitcast.44, f32[6144]{0:T(1024)S(1)} %bitcast.43, pred[224]{0:T(512)(128)(4,1)S(1)} %fusion), kind=kLoop, calls=%fused_computation | loop fusion | flops 5505024 | bytes 13811936 | tf_op jit(solution)/shard_map/broadcast_in_dim | solution.py:371
  (43 shorter events, 1.9 us)
Async XLA Ops:
  0.0 29.2 %copy-start = (s32[40,40]{1,0:T(8,128)S(1)}, s32[40,40]{1,0:T(8,128)}, u32[]{:S(2)}) copy-start(s32[40,40]{1,0:T(8,128)} %param.15) | copy-start | bytes 19204
  2.0 4.1 copy-start.3
  3.0 18.7 %collective-permute-start = (bf16[224,1536]{1,0:T(8,128)(2,1)}, bf16[224,1536]{1,0:T(8,128)(2,1)S(1)}, u32[]{:S(2)}, u32[]{:S(2)}) collective-permute-start(bf16[224,1536]{1,0:T(8,128)(2,1)} %dynamic-slice_bitcast_fusion.9), channel_id=1, source_target_pairs={{0,1},{1,0},{2,3},{3,2},{4,5},{5,4},{6,7},{7,6},{8,9},{9,8},{10,11... | collective-permute-start | bytes 2064392 | tf_op jit(solution)/shard_map/ppermute | solution.py:27
  26.1 59.6 %collective-permute-start.1 = (bf16[2,224,1536]{2,1,0:T(8,128)(2,1)}, bf16[2,224,1536]{2,1,0:T(8,128)(2,1)}, u32[]{:S(2)}, u32[]{:S(2)}) collective-permute-start(bf16[2,224,1536]{2,1,0:T(8,128)(2,1)} %pad_maximum_fusion), channel_id=1, source_target_pairs={{0,1},{1,0},{2,3},{3,2},{4,5},{5,4},{6,7},{7,6},{8,9},{9,8},{10,11... | collective-permute-start | bytes 4128776 | tf_op jit(solution)/shard_map/ppermute | solution.py:27
  29.6 141.8 %collective-permute-start.3 = (bf16[448,1536]{1,0:T(8,128)(2,1)S(1)}, bf16[448,1536]{1,0:T(8,128)(2,1)S(1)}, u32[]{:S(2)}, u32[]{:S(2)}) collective-permute-start(bf16[448,1536]{1,0:T(8,128)(2,1)S(1)} %constant_dynamic-update-slice_fusion.8.q_ref), channel_id=1, source_target_pairs={{0,2},{1,3},{2,0},{3,1},{4,6},{5,7},{6,4},{7,5},{8,10},{9,11},{10,... | collective-permute-start | bytes 4128776 | tf_op jit(solution)/shard_map/ppermute | solution.py:27
  91.3 113.4 %collective-permute-start.4 = (bf16[2,224,1536]{2,1,0:T(8,128)(2,1)S(1)}, bf16[2,224,1536]{2,1,0:T(8,128)(2,1)S(1)}, u32[]{:S(2)}, u32[]{:S(2)}) collective-permute-start(bf16[2,224,1536]{2,1,0:T(8,128)(2,1)S(1)} %pad_maximum_fusion.1), channel_id=1, source_target_pairs={{0,1},{1,0},{2,3},{3,2},{4,5},{5,4},{6,7},{7,6},{8,9},{9,8},{10,11... | collective-permute-start | bytes 4128776 | tf_op jit(solution)/shard_map/ppermute | solution.py:27
  91.5 79.5 %collective-permute-start.2 = (bf16[224,1536]{1,0:T(8,128)(2,1)S(1)}, bf16[224,1536]{1,0:T(8,128)(2,1)S(1)}, u32[]{:S(2)}, u32[]{:S(2)}) collective-permute-start(bf16[224,1536]{1,0:T(8,128)(2,1)S(1)} %dynamic-slice_bitcast_fusion.4), channel_id=1, source_target_pairs={{0,1},{1,0},{2,3},{3,2},{4,5},{5,4},{6,7},{7,6},{8,9},{9,8},{10,11... | collective-permute-start | bytes 2064392 | tf_op jit(solution)/shard_map/ppermute | solution.py:27
  100.3 111.4 %collective-permute-start.6 = (f32[12,448]{0,1:T(8,128)S(1)}, f32[12,448]{0,1:T(8,128)S(1)}, u32[]{:S(2)}, u32[]{:S(2)}) collective-permute-start(f32[12,448]{0,1:T(8,128)S(1)} %slice_bitcast_fusion), channel_id=1, source_target_pairs={{0,2},{1,3},{2,0},{3,1},{4,6},{5,7},{6,4},{7,5},{8,10},{9,11},{10,... | collective-permute-start | bytes 64520 | tf_op jit(solution)/shard_map/ppermute | solution.py:27
  101.3 110.8 %collective-permute-start.5 = (bf16[448,1536]{1,0:T(8,128)(2,1)S(1)}, bf16[448,1536]{1,0:T(8,128)(2,1)S(1)}, u32[]{:S(2)}, u32[]{:S(2)}) collective-permute-start(bf16[448,1536]{1,0:T(8,128)(2,1)S(1)} %get-tuple-element.18), channel_id=1, source_target_pairs={{0,2},{1,3},{2,0},{3,1},{4,6},{5,7},{6,4},{7,5},{8,10},{9,11},{10,... | collective-permute-start | bytes 4128776 | tf_op jit(solution)/shard_map/ppermute | solution.py:27
  212.3 5.0 %copy-start.4 = (f32[1,2,6144]{2,1,0:T(2,128)S(1)}, f32[1,2,6144]{2,1,0:T(2,128)}, u32[]{:S(2)}) copy-start(f32[1,2,6144]{2,1,0:T(2,128)} %param.12) | copy-start | bytes 147460
  215.7 1.5 copy-start.2
  217.3 192.9 %collective-permute-start.7 = (f32[224,6144]{1,0:T(8,128)}, f32[224,6144]{1,0:T(8,128)}, u32[]{:S(2)}, u32[]{:S(2)}) collective-permute-start(f32[224,6144]{1,0:T(8,128)} %bitcast.17), channel_id=1, source_target_pairs={{0,4},{4,8},{8,12},{12,16},{16,20},{20,24},{24,28},{28,0},{1,5},{5... | collective-permute-start | bytes 16515080 | tf_op jit(solution)/shard_map/ppermute | solution.py:32
  217.3 192.8 %collective-permute-start.8 = (f32[2,6144]{1,0:T(2,128)S(1)}, f32[2,6144]{1,0:T(2,128)S(1)}, u32[]{:S(2)}, u32[]{:S(2)}) collective-permute-start(f32[2,6144]{1,0:T(2,128)S(1)} %bitcast.45), channel_id=1, source_target_pairs={{0,4},{4,8},{8,12},{12,16},{16,20},{20,24},{24,28},{28,0},{1,5},{5... | collective-permute-start | bytes 147464 | tf_op jit(solution)/shard_map/ppermute | solution.py:32
  410.2 7.1 %copy-start.1 = (s32[40,40]{1,0:T(8,128)S(1)}, s32[40,40]{1,0:T(8,128)}, u32[]{:S(2)}) copy-start(s32[40,40]{1,0:T(8,128)} %param.15) | copy-start | bytes 19204

commit v6 on v5

--- a/solution.py
+++ b/solution.py
@@ -342,11 +342,11 @@
         return rows_gathered(cut, own_rows, place, group)
 
     across_q = gathered(True, (0,), qkv)
+    own_q = gathered(False, (0,), qkv)
     other_q = swapped(across_q, "sp", group)
     source, _ = lax.optimization_barrier((qkv, across_q))
     across_kv = gathered(True, (1, 2), source)
     source, _ = lax.optimization_barrier((qkv, across_kv))
-    own_q = gathered(False, (0,), source)
     own_kv = gathered(False, (1, 2), source)
 
     across_out, across_level = near_mix(across_q, across_kv)

time: 418 us -> 384 us (0.919)
  waiting for transfers between devices: 135 us -> 98.9 us
    ppermute x7, waiting for transfers between devices: 135 us -> 98.9 us  [swapped(): return lax.ppermute(shard, axis, [(i, i ^ bit) for i in range(devices)])]
  transfers between devices with their start and end apart: 9 -> 9, of which waited for: 3 -> 5; matrix products, arithmetic and copies ran while one was open for 2% -> 4% of each run, Pallas kernels for 57% -> 62%
where the time goes in v6:
time: 384 us; the launch traced here: 383 us
  Pallas kernels  242 us (63%)
  waiting for transfers between devices  98.9 us (26%)
  local copies, waits for them, and re-layouts  17.9 us (5%)
  starting transfers between devices  13.9 us (4%)
  other arithmetic  8.9 us (2%)
    pallas_call x1, Pallas kernels, summed_and_moved(): pl.pallas_call(lambda *refs: sum_kernel(devices, *refs), out_shape=jax.Sh...  192 us
    ppermute x7, waiting for transfers between devices, swapped(): return lax.ppermute(shard, axis, [(i, i ^ bit) for i in range(devices)])  98.9 us
    pallas_call x1, Pallas kernels, far_mix(): pl.pallas_call(far_kernel, grid=(VIDS, width // PAIR), in_specs=[block, p...  33.2 us
    pallas_call x2, Pallas kernels, near_mix(): pl.pallas_call(near_kernel, grid=(width // PAIR,), in_specs=[block, pl.Bl...  13.5 us
    ppermute x7, starting transfers between devices, swapped(): return lax.ppermute(shard, axis, [(i, i ^ bit) for i in range(devices)])  12.3 us
  transfers between devices with their start and end apart: 9, of which 5 were waited for; matrix products, arithmetic and copies ran while one was open for 4% of the time, Pallas kernels for 62%

profile of v6, /device:TPU:0, one launch (start us, length us, event | category | flops | bytes accessed | tf_op | source)
XLA Modules:
  0.0 383.1 jit_solution(10875299058307497530)
XLA Ops:
  0.0 2.0 slice.31
  2.0 1.1 dynamic-slice_bitcast_fusion.8
  3.1 3.0 collective-permute-start.1
  6.9 1.2 bitcast_dynamic-update-slice_fusion
  8.1 14.6 %collective-permute-done.1 = bf16[224,1536]{1,0:T(8,128)(2,1)} collective-permute-done((bf16[224,1536]{1,0:T(8,128)(2,1)}, bf16[224,1536]{1,0:T(8,128)(2,1)}, u32[]{:S(2)}, u32[]{:S(2)}) %collective-permute-start.1) | collective-permute-done | bytes 688160 | tf_op jit(solution)/shard_map/ppermute | solution.py:27
  22.7 1.1 constant_dynamic-update-slice_fusion.6.q_ref
  23.8 3.0 fusion.3
  26.8 0.2 dynamic-slice_bitcast_fusion.4
  27.0 1.2 pad_maximum_fusion
  28.2 2.1 collective-permute-start.3
  31.0 0.2 select_reduce_fusion
  31.4 1.2 bitcast_dynamic-update-slice_fusion.1
  32.6 2.7 collective-permute-start.2
  35.2 31.7 %collective-permute-done = bf16[224,1536]{1,0:T(8,128)(2,1)} collective-permute-done((bf16[224,1536]{1,0:T(8,128)(2,1)S(1)}, bf16[224,1536]{1,0:T(8,128)(2,1)}, u32[]{:S(2)}, u32[]{:S(2)}) %collective-permute-start) | collective-permute-done | bytes 688160 | tf_op jit(solution)/shard_map/ppermute | solution.py:27
  66.9 1.3 constant_dynamic-update-slice_fusion.8.q_ref
  68.2 0.2 broadcast.69.clone
  68.6 0.2 broadcast.67.clone
  68.9 26.7 %collective-permute-done.3 = bf16[2,224,1536]{2,1,0:T(8,128)(2,1)} collective-permute-done((bf16[2,224,1536]{2,1,0:T(8,128)(2,1)}, bf16[2,224,1536]{2,1,0:T(8,128)(2,1)}, u32[]{:S(2)}, u32[]{:S(2)}) %collective-permute-start.3) | collective-permute-done | bytes 1376288 | tf_op jit(solution)/shard_map/ppermute | solution.py:27
  95.6 1.5 constant_dynamic-update-slice_fusion.4.k_ref.v_ref
  97.1 0.5 fusion.2
  98.0 6.8 %shard_map.82 = (bf16[448,1536]{1,0:T(8,128)(2,1)S(1)}, f32[448,128]{1,0:T(8,128)S(1)}) custom-call(bf16[448,1536]{1,0:T(8,128)(2,1)S(1)} %constant_dynamic-update-slice_fusion.6.q_ref, bf16[2,448,1536]{2,1,0:T(8,128)(2,1)S(1)} %constant_dynamic-update-slice_fusion.4.k_ref.v_ref, bf16[2,448,1536]{2,1,0:T(8,128)(2,1)S(1)} %constant_dynamic-update-slice_fusion.4.k_ref.v_ref), custom_call_target="tpu_custom_call" | custom-call | flops 1233125376 | bytes 688128 | tf_op jit(solution)/shard_map/pallas_call | solution.py:132
  104.8 4.4 %collective-permute-start.6 = (f32[12,448]{0,1:T(8,128)S(1)}, f32[12,448]{0,1:T(8,128)S(1)}, u32[]{:S(2)}, u32[]{:S(2)}) collective-permute-start(f32[12,448]{0,1:T(8,128)S(1)} %slice_bitcast_fusion), channel_id=1, source_target_pairs={{0,2},{1,3},{2,0},{3,1},{4,6},{5,7},{6,4},{7,5},{8,10},{9,11},{10,... | collective-permute-start | bytes 64520 | tf_op jit(solution)/shard_map/ppermute | solution.py:27
  109.3 1.5 constant_dynamic-update-slice_fusion.5.q_ref
  111.1 33.2 %shard_map.83 = (f32[896,1536]{1,0:T(8,128)S(1)}, f32[896,128]{1,0:T(8,128)S(1)}) custom-call(bf16[896,1536]{1,0:T(8,128)(2,1)S(1)} %constant_dynamic-update-slice_fusion.5.q_ref, bf16[1,2,2,1344,1536]{4,3,2,1,0:T(8,128)(2,1)} %v_ref.1, bf16[1,2,2,1344,1536]{4,3,2,1,0:T(8,128)(2,1)} %v_ref.1, f32[8,1344]{1,0:T(8,128)S(1)} %broadcast_in_dim.75.bias_ref), custom_call_target="tpu_custom_call" | custom-call | flops 7398752256 | bytes 1376256 | tf_op jit(solution)/shard_map/pallas_call | solution.py:108
  144.3 7.5 %collective-permute-done.4 = bf16[2,224,1536]{2,1,0:T(8,128)(2,1)S(1)} collective-permute-done((bf16[2,224,1536]{2,1,0:T(8,128)(2,1)S(1)}, bf16[2,224,1536]{2,1,0:T(8,128)(2,1)S(1)}, u32[]{:S(2)}, u32[]{:S(2)}) %collective-permute-start.4) | collective-permute-done | bytes 1376288 | tf_op jit(solution)/shard_map/ppermute | solution.py:27
  151.9 6.8 %shard_map.84 = (bf16[448,1536]{1,0:T(8,128)(2,1)S(1)}, f32[448,128]{1,0:T(8,128)S(1)}) custom-call(bf16[448,1536]{1,0:T(8,128)(2,1)S(1)} %constant_dynamic-update-slice_fusion.8.q_ref, bf16[2,448,1536]{2,1,0:T(8,128)(2,1)S(1)} %constant_dynamic-update-slice_fusion.3.k_ref.v_ref, bf16[2,448,1536]{2,1,0:T(8,128)(2,1)S(1)} %constant_dynamic-update-slice_fusion.3.k_ref.v_ref), custom_call_target="tpu_custom_call" | custom-call | flops 1233125376 | bytes 688128 | tf_op jit(solution)/shard_map/pallas_call | solution.py:132
  159.2 18.5 %collective-permute-done.5 = bf16[448,1536]{1,0:T(8,128)(2,1)S(1)} collective-permute-done((bf16[448,1536]{1,0:T(8,128)(2,1)S(1)}, bf16[448,1536]{1,0:T(8,128)(2,1)S(1)}, u32[]{:S(2)}, u32[]{:S(2)}) %collective-permute-start.5) | collective-permute-done | bytes 1376288 | tf_op jit(solution)/shard_map/ppermute | solution.py:27
  177.8 3.5 shard_map.85.refs_0_
  181.2 1.5 copy-done.2
  182.8 1.7 collective-permute-start.8
  184.4 191.5 %shard_map.86 = bf16[224,6144]{1,0:T(8,128)(2,1)} custom-call(bf16[896,1536]{1,0:T(8,128)(2,1)} %copy-done.2, bf16[1,1536,6144]{2,1,0:T(8,128)(2,1)} %refs_1_.1), custom_call_target="tpu_custom_call" | custom-call | flops 16911433728 | bytes 18874368 | tf_op jit(solution)/shard_map/pallas_call | solution.py:281
  376.0 7.1 %add_bitcast_fusion = f32[1,224,6144]{2,1,0:T(8,128)} fusion(f32[224,6144]{1,0:T(8,128)} %collective-permute-done.7, bf16[224,6144]{1,0:T(8,128)(2,1)} %shard_map.86, f32[6144]{0:T(1024)S(1)} %bitcast.46, f32[6144]{0:T(1024)S(1)} %bitcast.45, pred[224]{0:T(512)(128)(4,1)S(1)} %fusion), kind=kLoop, calls=%fused_computation | loop fusion | flops 5505024 | bytes 13811936 | tf_op jit(solution)/shard_map/broadcast_in_dim | solution.py:371
  (47 shorter events, 2.3 us)
Async XLA Ops:
  0.0 30.3 %copy-start = (s32[40,40]{1,0:T(8,128)S(1)}, s32[40,40]{1,0:T(8,128)}, u32[]{:S(2)}) copy-start(s32[40,40]{1,0:T(8,128)} %param.15) | copy-start | bytes 19204
  2.0 4.8 %copy-start.3 = (bf16[1,224,1,6144]{3,1,2,0:T(8,128)(2,1)}, bf16[1,224,1,6144]{3,1,2,0:T(8,128)(2,1)S(1)}, u32[]{:S(2)}) copy-start(bf16[1,224,1,6144]{3,1,2,0:T(8,128)(2,1)S(1)} %slice.31) | copy-start | bytes 8257540
  3.1 19.6 %collective-permute-start.1 = (bf16[224,1536]{1,0:T(8,128)(2,1)}, bf16[224,1536]{1,0:T(8,128)(2,1)}, u32[]{:S(2)}, u32[]{:S(2)}) collective-permute-start(bf16[224,1536]{1,0:T(8,128)(2,1)} %get-tuple-element.39), channel_id=1, source_target_pairs={{0,1},{1,0},{2,3},{3,2},{4,5},{5,4},{6,7},{7,6},{8,9},{9,8},{10,11... | collective-permute-start | bytes 2064392 | tf_op jit(solution)/shard_map/ppermute | solution.py:27
  6.1 60.8 %collective-permute-start = (bf16[224,1536]{1,0:T(8,128)(2,1)S(1)}, bf16[224,1536]{1,0:T(8,128)(2,1)}, u32[]{:S(2)}, u32[]{:S(2)}) collective-permute-start(bf16[224,1536]{1,0:T(8,128)(2,1)S(1)} %get-tuple-element.40), channel_id=1, source_target_pairs={{0,1},{1,0},{2,3},{3,2},{4,5},{5,4},{6,7},{7,6},{8,9},{9,8},{10,11... | collective-permute-start | bytes 2064392 | tf_op jit(solution)/shard_map/ppermute | solution.py:27
  28.2 67.3 %collective-permute-start.3 = (bf16[2,224,1536]{2,1,0:T(8,128)(2,1)}, bf16[2,224,1536]{2,1,0:T(8,128)(2,1)}, u32[]{:S(2)}, u32[]{:S(2)}) collective-permute-start(bf16[2,224,1536]{2,1,0:T(8,128)(2,1)} %pad_maximum_fusion), channel_id=1, source_target_pairs={{0,1},{1,0},{2,3},{3,2},{4,5},{5,4},{6,7},{7,6},{8,9},{9,8},{10,11... | collective-permute-start | bytes 4128776 | tf_op jit(solution)/shard_map/ppermute | solution.py:27
  32.6 76.7 %collective-permute-start.2 = (bf16[448,1536]{1,0:T(8,128)(2,1)S(1)}, bf16[448,1536]{1,0:T(8,128)(2,1)}, u32[]{:S(2)}, u32[]{:S(2)}) collective-permute-start(bf16[448,1536]{1,0:T(8,128)(2,1)S(1)} %constant_dynamic-update-slice_fusion.6.q_ref), channel_id=1, source_target_pairs={{0,2},{1,3},{2,0},{3,1},{4,6},{5,7},{6,4},{7,5},{8,10},{9,11},{10,... | collective-permute-start | bytes 4128776 | tf_op jit(solution)/shard_map/ppermute | solution.py:27
  66.9 30.1 %slice-start = ((s8[8257536]{0:T(1024)(128)(4,1)}), s8[4194304]{0:T(1024)(128)(4,1)S(1)}, s32[]{:S(2)}) async-start(s8[8257536]{0:T(1024)(128)(4,1)} %bitcast.42), calls=%async_computation | async-start | bytes 8388608
  68.6 28.5 %slice-start.1 = ((s8[8257536]{0:T(1024)(128)(4,1)}), s8[4063232]{0:T(1024)(128)(4,1)S(1)}, s32[]{:S(2)}) async-start(s8[8257536]{0:T(1024)(128)(4,1)} %bitcast.42), calls=%async_computation.1 | async-start | bytes 8126464
  97.9 53.8 %collective-permute-start.4 = (bf16[2,224,1536]{2,1,0:T(8,128)(2,1)S(1)}, bf16[2,224,1536]{2,1,0:T(8,128)(2,1)S(1)}, u32[]{:S(2)}, u32[]{:S(2)}) collective-permute-start(bf16[2,224,1536]{2,1,0:T(8,128)(2,1)S(1)} %pad_maximum_fusion.1), channel_id=1, source_target_pairs={{0,1},{1,0},{2,3},{3,2},{4,5},{5,4},{6,7},{7,6},{8,9},{9,8},{10,11... | collective-permute-start | bytes 4128776 | tf_op jit(solution)/shard_map/ppermute | solution.py:27
  104.8 53.9 %collective-permute-start.6 = (f32[12,448]{0,1:T(8,128)S(1)}, f32[12,448]{0,1:T(8,128)S(1)}, u32[]{:S(2)}, u32[]{:S(2)}) collective-permute-start(f32[12,448]{0,1:T(8,128)S(1)} %slice_bitcast_fusion), channel_id=1, source_target_pairs={{0,2},{1,3},{2,0},{3,1},{4,6},{5,7},{6,4},{7,5},{8,10},{9,11},{10,... | collective-permute-start | bytes 64520 | tf_op jit(solution)/shard_map/ppermute | solution.py:27
  109.2 68.4 %collective-permute-start.5 = (bf16[448,1536]{1,0:T(8,128)(2,1)S(1)}, bf16[448,1536]{1,0:T(8,128)(2,1)S(1)}, u32[]{:S(2)}, u32[]{:S(2)}) collective-permute-start(bf16[448,1536]{1,0:T(8,128)(2,1)S(1)} %get-tuple-element.17), channel_id=1, source_target_pairs={{0,2},{1,3},{2,0},{3,1},{4,6},{5,7},{6,4},{7,5},{8,10},{9,11},{10,... | collective-permute-start | bytes 4128776 | tf_op jit(solution)/shard_map/ppermute | solution.py:27
  177.7 5.0 %copy-start.4 = (f32[1,2,6144]{2,1,0:T(2,128)S(1)}, f32[1,2,6144]{2,1,0:T(2,128)}, u32[]{:S(2)}) copy-start(f32[1,2,6144]{2,1,0:T(2,128)} %param.12) | copy-start | bytes 147460
  181.2 1.5 copy-start.2
  182.8 193.3 %collective-permute-start.7 = (f32[224,6144]{1,0:T(8,128)}, f32[224,6144]{1,0:T(8,128)}, u32[]{:S(2)}, u32[]{:S(2)}) collective-permute-start(f32[224,6144]{1,0:T(8,128)} %bitcast.17), channel_id=1, source_target_pairs={{0,4},{4,8},{8,12},{12,16},{16,20},{20,24},{24,28},{28,0},{1,5},{5... | collective-permute-start | bytes 16515080 | tf_op jit(solution)/shard_map/ppermute | solution.py:32
  182.8 193.2 %collective-permute-start.8 = (f32[2,6144]{1,0:T(2,128)S(1)}, f32[2,6144]{1,0:T(2,128)S(1)}, u32[]{:S(2)}, u32[]{:S(2)}) collective-permute-start(f32[2,6144]{1,0:T(2,128)S(1)} %bitcast.47), channel_id=1, source_target_pairs={{0,4},{4,8},{8,12},{12,16},{16,20},{20,24},{24,28},{28,0},{1,5},{5... | collective-permute-start | bytes 147464 | tf_op jit(solution)/shard_map/ppermute | solution.py:32
  376.0 7.1 %copy-start.1 = (s32[40,40]{1,0:T(8,128)S(1)}, s32[40,40]{1,0:T(8,128)}, u32[]{:S(2)}) copy-start(s32[40,40]{1,0:T(8,128)} %param.15) | copy-start | bytes 19204
